TPU v7x, 128 devices: a whole 4x4x4 slice. The times are simulated.
128 devices in a mesh: prompt: 4 (over y_hi, core), resp: 32 (over x, z, y_lo).
Axes of the slice: x: 4, y: 4 (y_hi: 2, y_lo: 2; y = y_hi * 2 + y_lo), z: 4, core: 2. Of those that a mesh axis runs over, the one named last changes fastest.
Arguments:
- prompt_keys: bfloat16 [512, 1024], P(('prompt', 'resp')), may hold values from -6 to 6
- prompt_values: bfloat16 [512, 1024], P(('prompt', 'resp')), may hold values from -24 to 24
- resp_queries: bfloat16 [16384, 8192], P('resp', 'prompt'), may hold values from -6 to 6
- resp_keys: bfloat16 [16384, 1024], P('resp', 'prompt'), may hold values from -6 to 6
- resp_values: bfloat16 [16384, 1024], P('resp', 'prompt'), may hold values from -24 to 24
- grad_out: bfloat16 [16384, 8192], P('resp', 'prompt'), may hold values from -24 to 24
- lengths: int32 [32], replicated, may hold values from 128 to 512, as said below
Outputs:
- attended: bfloat16 [16384, 8192], P('resp', 'prompt')
- query_grads: bfloat16 [16384, 8192], P('resp', 'prompt')
- key_grads: bfloat16 [16384, 1024], P('resp', 'prompt')
- value_grads: bfloat16 [16384, 1024], P('resp', 'prompt')
- prompt_key_grads: bfloat16 [512, 1024], P(('prompt', 'resp'))
- prompt_value_grads: bfloat16 [512, 1024], P(('prompt', 'resp'))
Inputs may be any that keep to these rules, and one draw needn't show every extreme that they name: `lengths`: each length is a multiple of 128, and some response has length 512 in every draw.
All inputs are finite; a program needn't handle non-finite values.
Results may differ from a plain program's by a relative error of at most 0.0092.
Values may be sent and summed in bfloat16 or wider, within the bound.
No kernel may reach another device: no remote copies, remote signals or barrier semaphores. Data moves between devices by JAX's collectives and lax.ppermute only.
A program may use at most 192 MiB of HBM per device.

v0:
```python
import math

import jax
import jax.numpy as jnp
from jax import lax
from jax.sharding import PartitionSpec as P

HD = 128


def group_pass(queries, keys, values, grads, allowed, live, scale):
    scores = jnp.einsum("thd,kd->thk", queries, keys, preferred_element_type=jnp.float32) * scale
    scores = jnp.where(allowed[:, None, :], scores, -1e30)
    peak = jnp.max(scores, axis=2, keepdims=True)
    exponent = jnp.exp(scores - peak)
    probs = exponent / jnp.sum(exponent, axis=2, keepdims=True)
    weights = probs.astype(jnp.bfloat16)
    mixed = jnp.einsum("thk,kd->thd", weights, values, preferred_element_type=jnp.float32)
    attended = jnp.where(live[:, None, None], mixed, 0.0).astype(jnp.bfloat16)
    drift = jnp.sum(grads.astype(jnp.float32) * mixed, axis=2, keepdims=True)
    prob_grads = jnp.einsum("thd,kd->thk", grads, values, preferred_element_type=jnp.float32)
    score_grads = (probs * (prob_grads - drift) * scale).astype(jnp.bfloat16)
    query_grads = jnp.einsum(
        "thk,kd->thd", score_grads, keys, preferred_element_type=jnp.float32
    ).astype(jnp.bfloat16)
    key_grads = jnp.einsum("thk,thd->kd", score_grads, queries, preferred_element_type=jnp.float32)
    value_grads = jnp.einsum("thk,thd->kd", weights, grads, preferred_element_type=jnp.float32)
    return (attended, query_grads, key_grads, value_grads)


def on_device(prompt_keys, prompt_values, resp_queries, resp_keys, resp_values, grad_out, lengths):
    row_count = resp_queries.shape[0]
    kv_width = resp_keys.shape[1]
    groups = kv_width // HD
    per_group = resp_queries.shape[1] // kv_width
    scale = 1.0 / math.sqrt(HD)
    position = lax.axis_index("resp")
    length = jnp.sum(jnp.where(jnp.arange(lengths.shape[0]) == position, lengths, 0))
    offsets = jnp.arange(row_count)
    live = offsets < length
    masked = jnp.where(live[:, None], grad_out, jnp.zeros_like(grad_out))
    split_k, split_v = (
        lax.all_to_all(prompt_keys, "prompt", split_axis=1, concat_axis=0, tiled=True),
        lax.all_to_all(prompt_values, "prompt", split_axis=1, concat_axis=0, tiled=True),
    )
    near_k, near_v = (
        lax.all_gather(split_k, "resp", axis=0, tiled=True),
        lax.all_gather(split_v, "resp", axis=0, tiled=True),
    )
    near_rows = near_k.shape[0]
    allowed = jnp.concatenate(
        [jnp.ones((row_count, near_rows), bool), offsets[None, :] <= offsets[:, None]], axis=1
    )
    attended_parts, query_parts = ([], [])
    prompt_kg, prompt_vg, own_kg, own_vg = ([], [], [], [])
    for group in range(groups):
        query_cols = slice(group * per_group * HD, (group + 1) * per_group * HD)
        key_cols = slice(group * HD, (group + 1) * HD)
        queries = resp_queries[:, query_cols].reshape(row_count, per_group, HD)
        grads = masked[:, query_cols].reshape(row_count, per_group, HD)
        keys = jnp.concatenate([near_k[:, key_cols], resp_keys[:, key_cols]], axis=0)
        values = jnp.concatenate([near_v[:, key_cols], resp_values[:, key_cols]], axis=0)
        attended, query_grads, key_grads, value_grads = group_pass(
            queries, keys, values, grads, allowed, live, scale
        )
        attended_parts.append(attended.reshape(row_count, per_group * HD))
        query_parts.append(query_grads.reshape(row_count, per_group * HD))
        prompt_kg.append(key_grads[:near_rows])
        prompt_vg.append(value_grads[:near_rows])
        own_kg.append(key_grads[near_rows:])
        own_vg.append(value_grads[near_rows:])
    key_out = jnp.concatenate(own_kg, axis=1).astype(jnp.bfloat16)
    value_out = jnp.concatenate(own_vg, axis=1).astype(jnp.bfloat16)
    prompt_key_terms = jnp.concatenate(prompt_kg, axis=1)
    prompt_value_terms = jnp.concatenate(prompt_vg, axis=1)
    part_k, part_v = (
        lax.psum_scatter(prompt_key_terms, "resp", scatter_dimension=0, tiled=True),
        lax.psum_scatter(prompt_value_terms, "resp", scatter_dimension=0, tiled=True),
    )
    summed_k, summed_v = (
        lax.all_to_all(part_k, "prompt", split_axis=0, concat_axis=1, tiled=True),
        lax.all_to_all(part_v, "prompt", split_axis=0, concat_axis=1, tiled=True),
    )
    return (
        jnp.concatenate(attended_parts, axis=1),
        jnp.concatenate(query_parts, axis=1),
        key_out,
        value_out,
        summed_k.astype(jnp.bfloat16),
        summed_v.astype(jnp.bfloat16),
    )


def solution(mesh):
    return jax.shard_map(
        on_device,
        mesh=mesh,
        in_specs=(
            P(("prompt", "resp"), None),
            P(("prompt", "resp"), None),
            P("resp", "prompt"),
            P("resp", "prompt"),
            P("resp", "prompt"),
            P("resp", "prompt"),
            P(),
        ),
        out_specs=(
            P("resp", "prompt"),
            P("resp", "prompt"),
            P("resp", "prompt"),
            P("resp", "prompt"),
            P(("prompt", "resp"), None),
            P(("prompt", "resp"), None),
        ),
        check_vma=False,
    )
```

profile of v0, /device:TPU:1, one launch (start us, length us, event | category | flops | bytes accessed | tf_op | source)
XLA Modules:
  0.0 640.5 jit_solution(266728297275602591)
XLA Ops:
  7.2 6.1 all-to-all-start
  13.3 1.4 fusion.16
  15.4 1.7 fusion.34
  17.1 1.8 broadcast_select_fusion
  18.9 1.2 fusion.29
  20.0 1.2 fusion.30
  21.2 4.8 all-to-all-start.1
  27.0 1.5 copy.94
  28.5 1.3 copy.100
  30.4 1.5 copy.147
  33.5 69.1 %all_gather.7 = bf16[512,256]{1,0:T(8,128)(2,1)S(1)} all-gather(bf16[16,256]{1,0:T(8,128)(2,1)S(1)} %all_to_all.55), channel_id=1, replica_groups=mesh['prompt'=4,'resp'=32] {'resp'}, dimensions={0}, use_global_device_ids=true | all-gather | bytes 270336 | tf_op jit(solution)/shard_map/all_gather | solution.py:48
  103.5 62.8 %all_gather.6 = bf16[512,256]{1,0:T(8,128)(2,1)S(1)} all-gather(bf16[16,256]{1,0:T(8,128)(2,1)S(1)} %all_to_all.51), channel_id=1, replica_groups=mesh['prompt'=4,'resp'=32] {'resp'}, dimensions={0}, use_global_device_ids=true | all-gather | bytes 270336 | tf_op jit(solution)/shard_map/all_gather | solution.py:47
  167.0 9.0 %fusion.12 = f32[1024,512,8]{1,0,2:T(8,128)} fusion(bf16[512,8,128]{0,2,1:T(8,128)(2,1)S(1)} %bitcast.98, bf16[512,128]{1,0:T(8,128)(2,1)} %get-tuple-element.35, bf16[512,128]{1,0:T(8,128)(2,1)S(1)} %get-tuple-element.33), kind=kOutput, calls=%fused_computation.46 | convolution fusion | flops 1074266112 | bytes 18087936 | tf_op jit(solution)/shard_map/thd,kd->thk/dot_general | solution.py:12
  176.0 18.0 %fusion.36 = (f32[512,8]{0,1:T(8,128)S(1)}, f32[512,8,1024]{0,2,1:T(8,128)}) fusion(f32[1024,512,8]{1,0,2:T(8,128)} %fusion.12, pred[512,1024]{0,1:T(8,128)(4,1)} %concatenate.35), kind=kOutput, calls=%fused_computation.72 | output fusion | flops 25166848 | bytes 34095104 | tf_op jit(solution)/shard_map/sub | solution.py:15
  194.0 7.5 %fusion.11 = bf16[512,8,1024]{0,2,1:T(8,128)(2,1)S(1)} fusion(f32[512,8,1024]{0,2,1:T(8,128)} %get-tuple-element.41, f32[512,8]{0,1:T(8,128)S(1)} %get-tuple-element.40), kind=kLoop, calls=%fused_computation.19 | loop fusion | flops 8388608 | bytes 25182208 | tf_op jit(solution)/shard_map/convert_element_type | solution.py:17
  201.6 4.2 copy-done
  205.8 2.2 multiply_reduce_fusion
  208.4 7.5 %multiply_convert_fusion = bf16[512,8,1024]{0,2,1:T(8,128)(2,1)} fusion(bf16[512,8,128]{0,2,1:T(8,128)(2,1)} %bitcast.102, f32[512,8]{0,1:T(8,128)S(1)} %get-tuple-element.43, f32[512,8,1024]{0,2,1:T(8,128)S(1)} %bitcast.95, f32[512,8]{0,1:T(8,128)S(1)} %get-tuple-element.40, bf16[512,128]{0,1:T(8,128)(2,1)S(1)} %copy-done.9, bf16[512,128]{0,1:T(8,128)(2,1)S(1)} %copy.145), kind=kOutput, calls=%fused_computation.4 | convolution fusion | flops 1095237632 | bytes 26509312 | tf_op jit(solution)/shard_map/thd,kd->thk/dot_general | solution.py:21
  215.9 6.2 convolution_bitcast_fusion.2
  222.9 8.1 %fusion.14 = f32[1024,512,8]{1,0,2:T(8,128)} fusion(bf16[512,8,128]{0,2,1:T(8,128)(2,1)S(1)} %bitcast.96, bf16[512,128]{1,0:T(8,128)(2,1)S(1)} %copy-done.11, bf16[512,128]{1,0:T(8,128)(2,1)S(1)} %copy-done.14), kind=kOutput, calls=%fused_computation.48 | convolution fusion | flops 1074266112 | bytes 18087936 | tf_op jit(solution)/shard_map/thd,kd->thk/dot_general | solution.py:12
  231.0 17.6 %fusion.35 = (f32[512,8]{0,1:T(8,128)S(1)}, f32[512,8,1024]{0,2,1:T(8,128)}) fusion(f32[1024,512,8]{1,0,2:T(8,128)} %fusion.14, pred[512,1024]{0,1:T(8,128)(4,1)S(1)} %copy-done.17), kind=kOutput, calls=%fused_computation.71 | output fusion | flops 25166848 | bytes 34095104 | tf_op jit(solution)/shard_map/sub | solution.py:15
  248.6 7.5 %fusion.10 = bf16[512,8,1024]{0,2,1:T(8,128)(2,1)S(1)} fusion(f32[512,8,1024]{0,2,1:T(8,128)} %get-tuple-element.39, f32[512,8]{0,1:T(8,128)S(1)} %get-tuple-element.38), kind=kLoop, calls=%fused_computation.18 | loop fusion | flops 8388608 | bytes 25182208 | tf_op jit(solution)/shard_map/convert_element_type | solution.py:17
  256.1 2.6 select_convert_fusion.1
  259.1 2.3 copy-done.1
  261.7 1.8 slice-done.3
  263.5 6.3 multiply_convert_fusion.1
  269.8 6.2 convolution_bitcast_fusion.3
  276.9 1.0 copy.138
  278.3 6.1 convolution_bitcast_fusion
  284.4 6.4 convolution_bitcast_fusion.1
  290.9 1.0 copy.140
  292.0 5.8 convolution_convert_fusion
  297.8 1.0 slice.104
  298.8 1.6 slice.105
  300.4 1.5 copy.107
  301.9 1.3 copy.92
  303.8 5.8 convolution_convert_fusion.1
  309.5 2.3 copy.106
  311.8 3.7 pad_maximum_fusion
  315.5 122.0 %reduce-scatter.7.cloned.1.call-done = f32[16,256]{1,0:T(8,128)} async-done(((f32[512,256]{1,0:T(8,128)}), f32[16,256]{1,0:T(8,128)}) %reduce-scatter.7.cloned.1.call-update) | async-done | bytes 16400 | tf_op jit(solution)/shard_map/reduce_scatter | solution.py:77
  437.6 1.3 all_to_all.56
  438.9 30.3 %all-to-all-start.2 = ((bf16[4,4,256]{2,1,0:T(4,128)(2,1)}), bf16[4,4,256]{2,1,0:T(4,128)(2,1)S(1)}, u32[]{:S(2)}, u32[]{:S(2)}) async-start(bf16[4,4,256]{2,1,0:T(4,128)(2,1)} %all_to_all.56), calls=%async_computation.2 | async-start | bytes 16384 | tf_op jit(solution)/shard_map/all_to_all | solution.py:81
  469.2 1.0 slice.102
  470.2 1.0 slice.103
  471.2 125.0 %reduce-scatter.9.cloned.1.call-done = f32[16,256]{1,0:T(8,128)} async-done(((f32[512,256]{1,0:T(8,128)}), f32[16,256]{1,0:T(8,128)}) %reduce-scatter.9.cloned.1.call-update) | async-done | bytes 16400 | tf_op jit(solution)/shard_map/reduce_scatter | solution.py:78
  596.1 1.3 all_to_all.58
  597.5 30.3 %all-to-all-start.3 = ((bf16[4,4,256]{2,1,0:T(4,128)(2,1)}), bf16[4,4,256]{2,1,0:T(4,128)(2,1)S(1)}, u32[]{:S(2)}, u32[]{:S(2)}) async-start(bf16[4,4,256]{2,1,0:T(4,128)(2,1)} %all_to_all.58), calls=%async_computation.3 | async-start | bytes 16384 | tf_op jit(solution)/shard_map/all_to_all | solution.py:82
  629.5 2.9 all-to-all-done.3
  (101 shorter events, 12.0 us)
Async XLA Ops:
  7.2 14.0 %copy-start.23 = (bf16[512,256]{1,0:T(8,128)(2,1)S(1)}, bf16[512,256]{1,0:T(8,128)(2,1)}, u32[]{:S(2)}) copy-start(bf16[512,256]{1,0:T(8,128)(2,1)} %param.11) | copy-start | bytes 786436
  7.2 14.1 %all-to-all-start = ((bf16[4,4,256]{2,0,1:T(4,128)(2,1)}), bf16[4,4,256]{2,0,1:T(4,128)(2,1)S(1)}, u32[]{:S(2)}, u32[]{:S(2)}) async-start(bf16[4,4,256]{2,0,1:T(4,128)(2,1)} %bitcast.111), calls=%async_computation | async-start | bytes 16384 | tf_op jit(solution)/shard_map/all_to_all | solution.py:43
  13.3 6.8 %copy-start.8 = (bf16[512,2048]{1,0:T(8,128)(2,1)S(1)}, bf16[512,2048]{1,0:T(8,128)(2,1)}, u32[]{:S(2)}) copy-start(bf16[512,2048]{1,0:T(8,128)(2,1)} %param.9) | copy-start | bytes 6291460
  15.4 11.6 %copy-start.24 = (pred[512]{0:T(512)(128)(4,1)}, pred[512]{0:T(512)(128)(4,1)S(1)}, u32[]{:S(2)}) copy-start(pred[512]{0:T(512)(128)(4,1)S(1)} %iota_compare_fusion.1) | copy-start | bytes 1540
  21.2 11.6 %all-to-all-start.1 = ((bf16[4,4,256]{2,0,1:T(4,128)(2,1)}), bf16[4,4,256]{2,0,1:T(4,128)(2,1)}, u32[]{:S(2)}, u32[]{:S(2)}) async-start(bf16[4,4,256]{2,0,1:T(4,128)(2,1)} %bitcast.5), calls=%async_computation.1 | async-start | bytes 16384 | tf_op jit(solution)/shard_map/all_to_all | solution.py:44
  26.1 411.5 %reduce-scatter.7.cloned.1.call-start = ((), (), s32[]{:S(2)}) async-start(), calls=%async_computation.6 | async-start | bytes 540672 | tf_op jit(solution)/shard_map/reduce_scatter | solution.py:77
  167.0 9.0 %copy-start.16 = (bf16[512,128]{1,0:T(8,128)(2,1)}, bf16[512,128]{1,0:T(8,128)(2,1)S(1)}, u32[]{:S(2)}) copy-start(bf16[512,128]{1,0:T(8,128)(2,1)S(1)} %get-tuple-element.33) | copy-start | bytes 393220
  194.0 11.8 %copy-start.2 = (bf16[512,1024]{0,1:T(8,128)(2,1)S(1)}, bf16[512,1024]{0,1:T(8,128)(2,1)}, u32[]{:S(2)}) copy-start(bf16[512,1024]{0,1:T(8,128)(2,1)} %copy.100) | copy-start | bytes 3145732
  194.0 11.8 %copy-start.9 = (bf16[512,128]{0,1:T(8,128)(2,1)S(1)}, bf16[512,128]{0,1:T(8,128)(2,1)}, u32[]{:S(2)}) copy-start(bf16[512,128]{0,1:T(8,128)(2,1)} %copy.146) | copy-start | bytes 393220
  194.0 14.1 %slice-start.4 = ((s8[16777216]{0:T(1024)(128)(4,1)}), s8[4194304]{0:T(1024)(128)(4,1)S(1)}, s32[]{:S(2)}) async-start(s8[16777216]{0:T(1024)(128)(4,1)} %bitcast.94), calls=%async_computation.12 | async-start | bytes 8388608
  194.0 14.1 %slice-start.5 = ((s8[16777216]{0:T(1024)(128)(4,1)}), s8[4194304]{0:T(1024)(128)(4,1)S(1)}, s32[]{:S(2)}) async-start(s8[16777216]{0:T(1024)(128)(4,1)} %bitcast.94), calls=%async_computation.13 | async-start | bytes 8388608
  194.0 14.1 %slice-start.6 = ((s8[16777216]{0:T(1024)(128)(4,1)}), s8[4194304]{0:T(1024)(128)(4,1)S(1)}, s32[]{:S(2)}) async-start(s8[16777216]{0:T(1024)(128)(4,1)} %bitcast.94), calls=%async_computation.14 | async-start | bytes 8388608
  201.6 4.3 copy-start
  205.8 2.5 slice-start.7
  215.9 7.0 %copy-start.11 = (bf16[512,128]{1,0:T(8,128)(2,1)S(1)}, bf16[512,128]{1,0:T(8,128)(2,1)}, u32[]{:S(2)}) copy-start(bf16[512,128]{1,0:T(8,128)(2,1)} %get-tuple-element.34) | copy-start | bytes 393220
  215.9 7.0 %copy-start.14 = (bf16[512,128]{1,0:T(8,128)(2,1)S(1)}, bf16[512,128]{1,0:T(8,128)(2,1)}, u32[]{:S(2)}) copy-start(bf16[512,128]{1,0:T(8,128)(2,1)} %get-tuple-element.32) | copy-start | bytes 393220
  222.1 0.8 copy-start.19
  222.9 8.1 %copy-start.17 = (pred[512,1024]{0,1:T(8,128)(4,1)S(1)}, pred[512,1024]{0,1:T(8,128)(4,1)}, u32[]{:S(2)}) copy-start(pred[512,1024]{0,1:T(8,128)(4,1)} %concatenate.35) | copy-start | bytes 1572868
  248.5 7.6 %copy-start.7 = (bf16[512,8,128]{0,2,1:T(8,128)(2,1)S(1)}, bf16[512,8,128]{0,2,1:T(8,128)(2,1)}, u32[]{:S(2)}) copy-start(bf16[512,8,128]{0,2,1:T(8,128)(2,1)} %get-tuple-element.44) | copy-start | bytes 3145732
  248.5 7.6 %copy-start.10 = (bf16[512,128]{0,1:T(8,128)(2,1)S(1)}, bf16[512,128]{0,1:T(8,128)(2,1)}, u32[]{:S(2)}) copy-start(bf16[512,128]{0,1:T(8,128)(2,1)} %copy.142) | copy-start | bytes 393220
  248.5 7.6 %copy-start.25 = (pred[512]{0:T(512)(128)(4,1)S(1)}, pred[512]{0:T(512)(128)(4,1)}, u32[]{:S(2)}) copy-start(pred[512]{0:T(512)(128)(4,1)} %copy-done.24) | copy-start | bytes 1540
  248.5 12.8 %slice-start = ((s8[16777216]{0:T(1024)(128)(4,1)}), s8[4194304]{0:T(1024)(128)(4,1)S(1)}, s32[]{:S(2)}) async-start(s8[16777216]{0:T(1024)(128)(4,1)} %bitcast.92), calls=%async_computation.8 | async-start | bytes 8388608
  248.5 12.8 %slice-start.1 = ((s8[16777216]{0:T(1024)(128)(4,1)}), s8[4194304]{0:T(1024)(128)(4,1)S(1)}, s32[]{:S(2)}) async-start(s8[16777216]{0:T(1024)(128)(4,1)} %bitcast.92), calls=%async_computation.9 | async-start | bytes 8388608
  248.6 13.2 %slice-start.2 = ((s8[16777216]{0:T(1024)(128)(4,1)}), s8[4194304]{0:T(1024)(128)(4,1)S(1)}, s32[]{:S(2)}) async-start(s8[16777216]{0:T(1024)(128)(4,1)} %bitcast.92), calls=%async_computation.10 | async-start | bytes 8388608
  256.1 5.3 copy-start.1
  256.1 7.4 %slice-start.3 = ((s8[16777216]{0:T(1024)(128)(4,1)}), s8[4194304]{0:T(1024)(128)(4,1)S(1)}, s32[]{:S(2)}) async-start(s8[16777216]{0:T(1024)(128)(4,1)} %bitcast.92), calls=%async_computation.11 | async-start | bytes 8388608
  269.8 8.4 %copy-start.3 = (bf16[512,1024]{0,1:T(8,128)(2,1)S(1)}, bf16[512,1024]{0,1:T(8,128)(2,1)}, u32[]{:S(2)}) copy-start(bf16[512,1024]{0,1:T(8,128)(2,1)} %copy.100) | copy-start | bytes 3145732
  276.0 0.8 copy-start.22
  277.9 318.2 %reduce-scatter.9.cloned.1.call-start = ((), (), s32[]{:S(2)}) async-start(), calls=%async_computation.7 | async-start | bytes 540672 | tf_op jit(solution)/shard_map/reduce_scatter | solution.py:78
  284.4 6.4 %copy-start.20 = (f32[1024,128]{0,1:T(8,128)}, f32[1024,128]{0,1:T(8,128)S(1)}, u32[]{:S(2)}) copy-start(f32[1024,128]{0,1:T(8,128)S(1)} %convolution_bitcast_fusion) | copy-start | bytes 1572868
  284.4 7.5 %copy-start.13 = (bf16[512,128]{1,0:T(8,128)(2,1)S(1)}, bf16[512,128]{1,0:T(8,128)(2,1)}, u32[]{:S(2)}) copy-start(bf16[512,128]{1,0:T(8,128)(2,1)} %get-tuple-element.35) | copy-start | bytes 393220
  290.8 1.1 copy-start.21
  291.9 10.0 %copy-start.5 = (bf16[512,8,128]{0,2,1:T(8,128)(2,1)S(1)}, bf16[512,8,128]{0,2,1:T(8,128)(2,1)}, u32[]{:S(2)}) copy-start(bf16[512,8,128]{0,2,1:T(8,128)(2,1)} %get-tuple-element.36) | copy-start | bytes 3145732
  291.9 11.3 %copy-start.4 = (bf16[512,8,128]{0,2,1:T(8,128)(2,1)S(1)}, bf16[512,8,128]{0,2,1:T(8,128)(2,1)}, u32[]{:S(2)}) copy-start(bf16[512,8,128]{0,2,1:T(8,128)(2,1)} %get-tuple-element.37) | copy-start | bytes 3145732
  291.9 11.8 %copy-start.12 = (bf16[512,128]{1,0:T(8,128)(2,1)S(1)}, bf16[512,128]{1,0:T(8,128)(2,1)}, u32[]{:S(2)}) copy-start(bf16[512,128]{1,0:T(8,128)(2,1)} %get-tuple-element.34) | copy-start | bytes 393220
  292.0 11.8 %copy-start.15 = (bf16[512,128]{1,0:T(8,128)(2,1)S(1)}, bf16[512,128]{1,0:T(8,128)(2,1)}, u32[]{:S(2)}) copy-start(bf16[512,128]{1,0:T(8,128)(2,1)} %get-tuple-element.32) | copy-start | bytes 393220
  303.8 8.1 %copy-start.6 = (bf16[512,1024]{1,0:T(8,128)(2,1)S(1)}, bf16[512,1024]{1,0:T(8,128)(2,1)}, u32[]{:S(2)}) copy-start(bf16[512,1024]{1,0:T(8,128)(2,1)} %copy.92) | copy-start | bytes 3145732
  309.5 159.7 %copy-start.18 = (bf16[512,128]{0,1:T(8,128)(2,1)S(1)}, bf16[512,128]{0,1:T(8,128)(2,1)}, u32[]{:S(2)}) copy-start(bf16[512,128]{0,1:T(8,128)(2,1)} %slice.105) | copy-start | bytes 393220
  438.9 158.6 %all-to-all-start.2 = ((bf16[4,4,256]{2,1,0:T(4,128)(2,1)}), bf16[4,4,256]{2,1,0:T(4,128)(2,1)S(1)}, u32[]{:S(2)}, u32[]{:S(2)}) async-start(bf16[4,4,256]{2,1,0:T(4,128)(2,1)} %all_to_all.56), calls=%async_computation.2 | async-start | bytes 16384 | tf_op jit(solution)/shard_map/all_to_all | solution.py:81
  597.5 35.0 %all-to-all-start.3 = ((bf16[4,4,256]{2,1,0:T(4,128)(2,1)}), bf16[4,4,256]{2,1,0:T(4,128)(2,1)S(1)}, u32[]{:S(2)}, u32[]{:S(2)}) async-start(bf16[4,4,256]{2,1,0:T(4,128)(2,1)} %all_to_all.58), calls=%async_computation.3 | async-start | bytes 16384 | tf_op jit(solution)/shard_map/all_to_all | solution.py:82
Sparse Core Ops, SparseCore 0:
  278.1 159.4 reduce-scatter.6
  440.0 156.0 reduce-scatter.8
where the time goes:
time: 641 us; the launch traced here: 640 us
  waiting for transfers between devices  250 us (39%)
  blocking collectives  132 us (21%)
  matrix products  72.2 us (11%)
  starting transfers between devices  71.9 us (11%)
  other arithmetic  58.7 us (9%)
  local copies, waits for them, and re-layouts  41.4 us (6%)
  between operations  14.5 us (2%)
    reduce_scatter x1, waiting for transfers between devices, on_device(): lax.psum_scatter(prompt_value_terms, 'resp', scatter_dimension=0, tiled=T...  125 us
    reduce_scatter x1, waiting for transfers between devices, on_device(): lax.psum_scatter(prompt_key_terms, 'resp', scatter_dimension=0, tiled=True)  122 us
    all_gather x1, blocking collectives, on_device(): lax.all_gather(split_v, 'resp', axis=0, tiled=True)  69.1 us
    all_gather x1, blocking collectives, on_device(): lax.all_gather(split_k, 'resp', axis=0, tiled=True)  62.8 us
    sub x2, other arithmetic, group_pass(): exponent = jnp.exp(scores - peak)  35.5 us
    all_to_all x1, starting transfers between devices, on_device(): lax.all_to_all(part_v, 'prompt', split_axis=0, concat_axis=1, tiled=True)  30.3 us
    all_to_all x1, starting transfers between devices, on_device(): lax.all_to_all(part_k, 'prompt', split_axis=0, concat_axis=1, tiled=True)  30.3 us
    unnamed x80, local copies, waits for them, and re-layouts  19.3 us
  transfers between devices with their start and end apart: 6, of which 3 were waited for; matrix products, arithmetic and copies ran while one was open for 9% of the time, Pallas kernels for 0%

commit v1 on v0

v1 whole, which is shorter than its diff:
```python
import functools
import math

import jax
import jax.numpy as jnp
from jax import lax
from jax.experimental import pallas as pl
from jax.experimental.pallas import tpu as pltpu
from jax.sharding import PartitionSpec as P

HD = 128
BLK = 256
SCALE = 1.0 / math.sqrt(HD)
EXP_SCALE = SCALE * math.log2(math.e)
NEG = -1e30
F32 = jnp.float32
BF16 = jnp.bfloat16


def dot_nt(a, b):
    return lax.dot_general(a, b, (((1,), (1,)), ((), ())), preferred_element_type=F32)


def dot_nn(a, b):
    return lax.dot_general(a, b, (((1,), (0,)), ((), ())), preferred_element_type=F32)


def live_rows(block, start, length):
    parts = []
    for at in range(0, block.shape[0], HD):
        factor = (start + at < length).astype(F32).astype(BF16)
        parts.append(block[at : at + HD] * factor)
    return jnp.concatenate(parts, axis=0)


def causal(s):
    key = lax.broadcasted_iota(jnp.int32, s.shape, 0)
    query = lax.broadcasted_iota(jnp.int32, s.shape, 1)
    return jnp.where(key <= query, s, NEG)


def own_scores(k, q, at):
    s = dot_nt(k[: at + BLK], q)
    tail = causal(s[at:])
    return tail if at == 0 else jnp.concatenate([s[:at], tail], axis=0)


def own_forward(q_ref, k_ref, v_ref, mixed_ref, stats_ref, vt_ref, *, per_group):
    @pl.when(pl.program_id(0) % per_group == 0)
    def _():
        vt_ref[...] = v_ref[...].T

    rows = q_ref.shape[0]
    for at in range(0, rows, BLK):
        s = own_scores(k_ref[...], q_ref[at : at + BLK, :], at)
        peak = jnp.max(s, axis=0, keepdims=True)
        e = jnp.exp2((s - peak) * EXP_SCALE)
        total = jnp.sum(e, axis=0, keepdims=True)
        mixed_ref[0, :, at : at + BLK] = dot_nn(vt_ref[:, : at + BLK], e.astype(BF16))
        stats_ref[0, 0:1, at : at + BLK] = peak
        stats_ref[0, 1:2, at : at + BLK] = total


def shared_pass(
    length_ref, q_ref, g_ref, k_ref, v_ref, mixed_ref, stats_ref,
    att_ref, qg_ref, back_ref, kg_ref, vg_ref, kt_ref, vt_ref, *, per_group
):
    length = length_ref[0]
    rows = q_ref.shape[0]

    @pl.when(pl.program_id(0) % per_group == 0)
    def _():
        kt_ref[...] = k_ref[0].T
        vt_ref[...] = v_ref[0].T
        kg_ref[...] = jnp.zeros_like(kg_ref)
        vg_ref[...] = jnp.zeros_like(vg_ref)

    keys, values = k_ref[0], v_ref[0]
    for at in range(0, rows, BLK):
        cols = slice(at, at + BLK)
        q = q_ref[cols, :]
        g = live_rows(g_ref[cols, :], at, length)
        s = dot_nt(keys, q)
        own_peak = stats_ref[0, 0:1, cols]
        peak = jnp.maximum(jnp.max(s, axis=0, keepdims=True), own_peak)
        e = jnp.exp2((s - peak) * EXP_SCALE)
        decay = jnp.exp2((own_peak - peak) * EXP_SCALE)
        total = jnp.sum(e, axis=0, keepdims=True) + stats_ref[0, 1:2, cols] * decay
        inverse = 1.0 / total
        p = e * inverse
        w = p.astype(BF16)
        mixed = dot_nn(vt_ref[...], w) + mixed_ref[0, :, cols] * (decay * inverse)
        live = lax.broadcasted_iota(jnp.int32, (1, BLK), 1) + at < length
        att_ref[cols, :] = jnp.where(live, mixed, 0.0).T.astype(BF16)
        drift = jnp.sum(g.T.astype(F32) * mixed, axis=0, keepdims=True)
        dp = dot_nt(values, g)
        ds = (p * (dp - drift) * SCALE).astype(BF16)
        qg_ref[0, :, cols] = dot_nn(kt_ref[...], ds)
        kg_ref[0] += dot_nn(ds, q)
        vg_ref[0] += dot_nn(w, g)
        back_ref[0, 0:1, cols] = peak
        back_ref[0, 1:2, cols] = inverse
        back_ref[0, 2:3, cols] = drift


def own_backward(
    length_ref, q_ref, g_ref, k_ref, v_ref, part_ref, back_ref,
    qg_ref, kg_ref, vg_ref, kt_ref, kacc_ref, vacc_ref, *, per_group
):
    length = length_ref[0]
    rows = q_ref.shape[0]
    head = pl.program_id(0) % per_group

    @pl.when(head == 0)
    def _():
        kt_ref[...] = k_ref[...].T
        kacc_ref[...] = jnp.zeros_like(kacc_ref)
        vacc_ref[...] = jnp.zeros_like(vacc_ref)

    for at in range(0, rows, BLK):
        cols = slice(at, at + BLK)
        upto = slice(0, at + BLK)
        q = q_ref[cols, :]
        g = live_rows(g_ref[cols, :], at, length)
        s = own_scores(k_ref[...], q, at)
        p = jnp.exp2((s - back_ref[0, 0:1, cols]) * EXP_SCALE) * back_ref[0, 1:2, cols]
        w = p.astype(BF16)
        dp = dot_nt(v_ref[upto, :], g)
        ds = (p * (dp - back_ref[0, 2:3, cols]) * SCALE).astype(BF16)
        qg = dot_nn(kt_ref[:, upto], ds) + part_ref[0, :, cols]
        qg_ref[cols, :] = qg.T.astype(BF16)
        kacc_ref[upto, :] += dot_nn(ds, q)
        vacc_ref[upto, :] += dot_nn(w, g)

    @pl.when(head == per_group - 1)
    def _():
        kg_ref[...] = kacc_ref[...].astype(BF16)
        vg_ref[...] = vacc_ref[...].astype(BF16)


VMEM_LIMIT = 48 * 2**20


def params():
    return pltpu.CompilerParams(
        dimension_semantics=("arbitrary",), vmem_limit_bytes=VMEM_LIMIT
    )


def shape(dims, dtype=F32):
    return jax.ShapeDtypeStruct(dims, dtype)


def run_own_forward(q, k, v):
    rows, width = q.shape
    heads, groups = width // HD, k.shape[1] // HD
    per_group = heads // groups
    return pl.pallas_call(
        functools.partial(own_forward, per_group=per_group),
        grid=(heads,),
        in_specs=[
            pl.BlockSpec((rows, HD), lambda h: (0, h)),
            pl.BlockSpec((rows, HD), lambda h: (0, h // per_group)),
            pl.BlockSpec((rows, HD), lambda h: (0, h // per_group)),
        ],
        out_specs=[
            pl.BlockSpec((1, HD, rows), lambda h: (h, 0, 0)),
            pl.BlockSpec((1, 8, rows), lambda h: (h, 0, 0)),
        ],
        out_shape=[shape((heads, HD, rows)), shape((heads, 8, rows))],
        scratch_shapes=[pltpu.VMEM((HD, rows), BF16)],
        compiler_params=params(),
        cost_estimate=pl.CostEstimate(
            flops=3 * heads * rows * rows * HD, bytes_accessed=8 * 2**20, transcendentals=0
        ),
        name="own_forward",
    )(q, k, v)


def run_shared(length, q, g, k, v, mixed, stats):
    rows, width = q.shape
    heads, groups = width // HD, k.shape[0]
    near = k.shape[1]
    per_group = heads // groups
    head_block = pl.BlockSpec((rows, HD), lambda h: (0, h))
    group_block = pl.BlockSpec((1, near, HD), lambda h: (h // per_group, 0, 0))
    wide_block = pl.BlockSpec((1, HD, rows), lambda h: (h, 0, 0))
    stat_block = pl.BlockSpec((1, 8, rows), lambda h: (h, 0, 0))
    return pl.pallas_call(
        functools.partial(shared_pass, per_group=per_group),
        grid=(heads,),
        in_specs=[
            pl.BlockSpec(memory_space=pltpu.SMEM),
            head_block, head_block, group_block, group_block, wide_block, stat_block,
        ],
        out_specs=[head_block, wide_block, stat_block, group_block, group_block],
        out_shape=[
            shape((rows, width), BF16), shape((heads, HD, rows)), shape((heads, 8, rows)),
            shape((groups, near, HD)), shape((groups, near, HD)),
        ],
        scratch_shapes=[pltpu.VMEM((HD, near), BF16)] * 2,
        compiler_params=params(),
        cost_estimate=pl.CostEstimate(
            flops=12 * heads * rows * near * HD, bytes_accessed=16 * 2**20, transcendentals=0
        ),
        name="shared_pass",
    )(length, q, g, k, v, mixed, stats)


def run_own_backward(length, q, g, k, v, part, back):
    rows, width = q.shape
    heads, groups = width // HD, k.shape[1] // HD
    per_group = heads // groups
    head_block = pl.BlockSpec((rows, HD), lambda h: (0, h))
    group_block = pl.BlockSpec((rows, HD), lambda h: (0, h // per_group))
    return pl.pallas_call(
        functools.partial(own_backward, per_group=per_group),
        grid=(heads,),
        in_specs=[
            pl.BlockSpec(memory_space=pltpu.SMEM),
            head_block, head_block, group_block, group_block,
            pl.BlockSpec((1, HD, rows), lambda h: (h, 0, 0)),
            pl.BlockSpec((1, 8, rows), lambda h: (h, 0, 0)),
        ],
        out_specs=[head_block, group_block, group_block],
        out_shape=[shape((rows, width), BF16), shape(k.shape, BF16), shape(v.shape, BF16)],
        scratch_shapes=[
            pltpu.VMEM((HD, rows), BF16), pltpu.VMEM((rows, HD), F32), pltpu.VMEM((rows, HD), F32)
        ],
        compiler_params=params(),
        cost_estimate=pl.CostEstimate(
            flops=8 * heads * rows * rows * HD, bytes_accessed=12 * 2**20, transcendentals=0
        ),
        name="own_backward",
    )(length, q, g, k, v, part, back)


def on_device(prompt_keys, prompt_values, q, resp_k, resp_v, grad_out, lengths):
    axes = ("prompt", "resp")
    shares = lax.axis_size("prompt")
    copies = lax.axis_size("resp")
    tokens = prompt_keys.shape[0]
    groups = resp_k.shape[1] // HD
    near = tokens * shares * copies
    length = lax.dynamic_slice(lengths, (lax.axis_index("resp"),), (1,))

    pieces = jnp.stack([prompt_keys, prompt_values], axis=1)
    pieces = pieces.reshape(tokens, 2, shares, groups, HD).transpose(2, 0, 1, 3, 4)
    pieces = jnp.broadcast_to(pieces[:, None], (shares, copies) + pieces.shape[1:])
    pieces = pieces.reshape(shares * copies, tokens * 2 * groups, HD)
    arrived = lax.all_to_all(pieces, axes, split_axis=0, concat_axis=0, tiled=True)
    arrived = arrived.reshape(near, 2, groups, HD).transpose(1, 2, 0, 3)

    mixed, stats = run_own_forward(q, resp_k, resp_v)
    attended, part, back, kg, vg = run_shared(
        length, q, grad_out, arrived[0], arrived[1], mixed, stats
    )
    terms = jnp.stack([kg, vg]).transpose(2, 0, 1, 3).astype(BF16)
    terms = terms.reshape(shares * copies, tokens * 2 * groups, HD)
    terms = lax.all_to_all(terms, axes, split_axis=0, concat_axis=0, tiled=True)
    query_grads, key_grads, value_grads = run_own_backward(
        length, q, grad_out, resp_k, resp_v, part, back
    )
    terms = terms.reshape(shares, copies, tokens, 2, groups, HD).astype(F32)
    sums = jnp.sum(terms, axis=1).transpose(2, 1, 0, 3, 4)
    sums = sums.reshape(2, tokens, shares * groups * HD).astype(BF16)
    return attended, query_grads, key_grads, value_grads, sums[0], sums[1]


def solution(mesh):
    return jax.shard_map(
        on_device,
        mesh=mesh,
        in_specs=(
            P(("prompt", "resp"), None),
            P(("prompt", "resp"), None),
            P("resp", "prompt"),
            P("resp", "prompt"),
            P("resp", "prompt"),
            P("resp", "prompt"),
            P(),
        ),
        out_specs=(
            P("resp", "prompt"),
            P("resp", "prompt"),
            P("resp", "prompt"),
            P("resp", "prompt"),
            P(("prompt", "resp"), None),
            P(("prompt", "resp"), None),
        ),
        check_vma=False,
    )
```

time: 641 us -> 106 us (0.17)
  waiting for transfers between devices: 250 us -> 0.01 us
  blocking collectives: 132 us -> 0 us
  matrix products: 72.2 us -> 0 us
  Pallas kernels: 0 us -> 69.8 us
  other arithmetic: 58.7 us -> 0.58 us
  starting transfers between devices: 71.9 us -> 21.3 us
  local copies, waits for them, and re-layouts: 41.4 us -> 13 us
  between operations: 14.5 us -> 0.75 us
    reduce_scatter x2 -> x0, waiting for transfers between devices: 247 us -> none  [the longest x1 125 us: on_device(): lax.psum_scatter(prompt_value_terms, 'resp', scatter_dimension=0, tiled=T...]
    all_gather x2 -> x0, blocking collectives: 132 us -> none  [the longest x1 69.1 us: on_device(): lax.all_gather(split_v, 'resp', axis=0, tiled=True)]
    dot_general x12 -> x0, matrix products: 72.2 us -> none  [the longest x2 17.1 us: group_pass(): jnp.einsum('thd,kd->thk', queries, keys, preferred_element_type=jnp.float32)]
    pallas_call x0 -> x3, Pallas kernels: none -> 69.8 us  [the longest x1 35.3 us: run_shared(): pl.pallas_call(functools.partial(shared_pass, per_group=per_group), grid=...]
    all_to_all x4 -> x2, starting transfers between devices: 71.6 us -> 21.3 us  [the longest x1 11.5 us: on_device(): lax.all_to_all(pieces, axes, split_axis=0, concat_axis=0, tiled=True)]
    sub x2 -> x0, other arithmetic: 35.5 us -> none  [group_pass(): exponent = jnp.exp(scores - peak)]
    convert_element_type x2 -> x1, other arithmetic: 15 us -> 0.05 us  [on_device(): terms = jnp.stack([kg, vg]).transpose(2, 0, 1, 3).astype(BF16)]
    unnamed x80 -> x14, local copies, waits for them, and re-layouts: 19.3 us -> 6.55 us
  transfers between devices with their start and end apart: 6 -> 2, of which waited for: 3 -> 0; matrix products, arithmetic and copies ran while one was open for 9% -> 1% of each run, Pallas kernels for 0% -> 33%
where the time goes in v1:
time: 106 us; the launch traced here: 105 us
  Pallas kernels  69.8 us (66%)
  starting transfers between devices  21.3 us (20%)
  local copies, waits for them, and re-layouts  13 us (12%)
    pallas_call x1, Pallas kernels, run_shared(): pl.pallas_call(functools.partial(shared_pass, per_group=per_group), grid=...  35.3 us
    pallas_call x1, Pallas kernels, run_own_backward(): pl.pallas_call(functools.partial(own_backward, per_group=per_group), grid...  19.4 us
    pallas_call x1, Pallas kernels, run_own_forward(): pl.pallas_call(functools.partial(own_forward, per_group=per_group), grid=...  15 us
    all_to_all x1, starting transfers between devices, on_device(): lax.all_to_all(pieces, axes, split_axis=0, concat_axis=0, tiled=True)  11.5 us
    all_to_all x1, starting transfers between devices, on_device(): terms = lax.all_to_all(terms, axes, split_axis=0, concat_axis=0, tiled=True)  9.76 us
    unnamed x14, local copies, waits for them, and re-layouts  6.55 us
  transfers between devices with their start and end apart: 2, of which 0 were waited for; matrix products, arithmetic and copies ran while one was open for 1% of the time, Pallas kernels for 33%

profile of v1, /device:TPU:1, one launch (start us, length us, event | category | flops | bytes accessed | tf_op | source)
XLA Modules:
  0.0 105.3 jit_solution(8859857414139190171)
XLA Ops:
  0.6 0.7 stack.21
  1.3 0.7 stack.22
  2.1 1.1 %broadcast_in_dim.2 = bf16[4,32,4,2,2,128]{5,4,3,2,1,0:T(2,128)(2,1)} broadcast(bf16[4,4,2,2,128]{4,3,2,1,0:T(2,128)(2,1)S(1)} %copy.20), dimensions={0,2,3,4,5} | broadcast | bytes 540672 | tf_op jit(solution)/shard_map/broadcast_in_dim | solution.py:249
  3.2 11.5 %all-to-all-start = ((bf16[128,16,128]{2,1,0:T(8,128)(2,1)}), bf16[128,16,128]{2,1,0:T(8,128)(2,1)S(1)}, u32[]{:S(2)}, u32[]{:S(2)}) async-start(bf16[128,16,128]{2,1,0:T(8,128)(2,1)} %bitcast.1), calls=%async_computation | async-start | bytes 1048576 | tf_op jit(solution)/shard_map/all_to_all | solution.py:251
  14.7 1.2 %dynamic_slice.3.length_ref = s32[1]{0:T(128)} dynamic-slice(s32[32]{0:T(128)} %param.13, s32[]{:T(128)S(6)} %select_n.3), dynamic_slice_sizes={1} | dynamic-slice | bytes 12 | tf_op jit(solution)/shard_map/dynamic_slice | solution.py:245
  15.9 0.0 copy-start
  15.9 1.6 %copy-done = bf16[512,2048]{1,0:T(8,128)(2,1)S(1)} copy-done((bf16[512,2048]{1,0:T(8,128)(2,1)S(1)}, bf16[512,2048]{1,0:T(8,128)(2,1)}, u32[]{:S(2)}) %copy-start) | copy-done | bytes 2097176
  17.5 0.0 copy-start.3
  17.5 0.9 copy-done.3
  18.5 0.0 copy-start.5
  18.5 0.9 copy-done.5
  19.4 15.0 %own_forward.1 = (f32[16,128,512]{2,1,0:T(8,128)}, f32[16,8,512]{2,1,0:T(8,128)S(1)}) custom-call(bf16[512,2048]{1,0:T(8,128)(2,1)S(1)} %copy-done, bf16[512,256]{1,0:T(8,128)(2,1)S(1)} %copy-done.3, bf16[512,256]{1,0:T(8,128)(2,1)S(1)} %copy-done.5), custom_call_target="tpu_custom_call" | custom-call | flops 1610612736 | bytes 8388608 | tf_op jit(solution)/shard_map/own_forward/pallas_call | solution.py:158
  34.5 0.0 copy-start.1
  34.5 0.0 all-to-all-done
  34.5 0.1 copy.26
  34.6 1.5 %copy-done.1 = bf16[512,2048]{1,0:T(8,128)(2,1)S(1)} copy-done((bf16[512,2048]{1,0:T(8,128)(2,1)S(1)}, bf16[512,2048]{1,0:T(8,128)(2,1)}, u32[]{:S(2)}) %copy-start.1) | copy-done | bytes 2097176
  36.0 35.3 %shared_pass.1 = (bf16[512,2048]{1,0:T(8,128)(2,1)}, f32[16,128,512]{2,1,0:T(8,128)}, f32[16,8,512]{2,1,0:T(8,128)S(1)}, f32[2,512,128]{2,1,0:T(8,128)S(1)}, f32[2,512,128]{2,1,0:T(8,128)S(1)}) custom-call(s32[1]{0:T(128)} %dynamic_slice.3.length_ref, bf16[512,2048]{1,0:T(8,128)(2,1)S(1)} %copy-done.1, bf16[512,2048]{1,0:T(8,128)(2,1)} %g_ref.3, ...), custom_call_target="tpu_custom_call" | custom-call | flops 6442450944 | bytes 16777216 | tf_op jit(solution)/shard_map/shared_pass/pallas_call | solution.py:189
  71.4 0.0 copy-start.4
  71.4 0.0 copy-start.6
  71.4 0.1 convert_bitcast_fusion
  71.5 0.1 maximum_bitcast_fusion
  71.5 1.3 %copy.22 = bf16[512,2,2,128]{3,2,1,0:T(2,128)(2,1)} copy(bf16[512,2,2,128]{3,0,2,1:T(8,128)(2,1)S(1)} %maximum_bitcast_fusion) | data formatting | bytes 1048576 | tf_op jit(solution)/shard_map/convert_element_type | solution.py:258
  72.9 9.8 %all-to-all-start.1 = ((bf16[128,16,128]{2,1,0:T(8,128)(2,1)}), bf16[128,16,128]{2,1,0:T(8,128)(2,1)S(1)}, u32[]{:S(2)}, u32[]{:S(2)}) async-start(bf16[128,16,128]{2,1,0:T(8,128)(2,1)} %bitcast.22), calls=%async_computation.1 | async-start | bytes 1048576 | tf_op jit(solution)/shard_map/all_to_all | solution.py:260
  82.6 0.0 copy-done.4
  82.7 0.0 copy-done.6
  82.7 0.0 copy-start.2
  82.7 1.6 %copy-done.2 = bf16[512,2048]{1,0:T(8,128)(2,1)S(1)} copy-done((bf16[512,2048]{1,0:T(8,128)(2,1)S(1)}, bf16[512,2048]{1,0:T(8,128)(2,1)}, u32[]{:S(2)}) %copy-start.2) | copy-done | bytes 2097176
  84.3 19.4 %own_backward.1 = (bf16[512,2048]{1,0:T(8,128)(2,1)}, bf16[512,256]{1,0:T(8,128)(2,1)}, bf16[512,256]{1,0:T(8,128)(2,1)}) custom-call(s32[1]{0:T(128)} %dynamic_slice.3.length_ref, bf16[512,2048]{1,0:T(8,128)(2,1)S(1)} %copy-done.1, bf16[512,2048]{1,0:T(8,128)(2,1)S(1)} %copy-done.2, bf16[512,256]{1,0:T(8,128)(2,1)S(1)} %copy-done.4, ...), custom_call_target="tpu_custom_call" | custom-call | flops 4294967296 | bytes 12582912 | tf_op jit(solution)/shard_map/own_backward/pallas_call | solution.py:216
  103.6 0.0 all-to-all-done.1
  103.6 0.4 reduce
  104.1 0.6 squeeze.15
  104.7 0.6 squeeze.14
  (6 shorter events, 0.1 us)
Async XLA Ops:
  3.2 31.3 %all-to-all-start = ((bf16[128,16,128]{2,1,0:T(8,128)(2,1)}), bf16[128,16,128]{2,1,0:T(8,128)(2,1)S(1)}, u32[]{:S(2)}, u32[]{:S(2)}) async-start(bf16[128,16,128]{2,1,0:T(8,128)(2,1)} %bitcast.1), calls=%async_computation | async-start | bytes 1048576 | tf_op jit(solution)/shard_map/all_to_all | solution.py:251
  15.9 1.6 %copy-start = (bf16[512,2048]{1,0:T(8,128)(2,1)S(1)}, bf16[512,2048]{1,0:T(8,128)(2,1)}, u32[]{:S(2)}) copy-start(bf16[512,2048]{1,0:T(8,128)(2,1)} %q_ref.5) | copy-start | bytes 6291460
  17.5 0.9 copy-start.3
  18.5 0.9 copy-start.5
  34.5 1.6 %copy-start.1 = (bf16[512,2048]{1,0:T(8,128)(2,1)S(1)}, bf16[512,2048]{1,0:T(8,128)(2,1)}, u32[]{:S(2)}) copy-start(bf16[512,2048]{1,0:T(8,128)(2,1)} %q_ref.5) | copy-start | bytes 6291460
  71.4 11.3 %copy-start.4 = (bf16[512,256]{1,0:T(8,128)(2,1)S(1)}, bf16[512,256]{1,0:T(8,128)(2,1)}, u32[]{:S(2)}) copy-start(bf16[512,256]{1,0:T(8,128)(2,1)} %k_ref.3) | copy-start | bytes 786436
  71.4 11.3 %copy-start.6 = (bf16[512,256]{1,0:T(8,128)(2,1)S(1)}, bf16[512,256]{1,0:T(8,128)(2,1)}, u32[]{:S(2)}) copy-start(bf16[512,256]{1,0:T(8,128)(2,1)} %v_ref.3) | copy-start | bytes 786436
  72.9 30.8 %all-to-all-start.1 = ((bf16[128,16,128]{2,1,0:T(8,128)(2,1)}), bf16[128,16,128]{2,1,0:T(8,128)(2,1)S(1)}, u32[]{:S(2)}, u32[]{:S(2)}) async-start(bf16[128,16,128]{2,1,0:T(8,128)(2,1)} %bitcast.22), calls=%async_computation.1 | async-start | bytes 1048576 | tf_op jit(solution)/shard_map/all_to_all | solution.py:260
  82.7 1.6 %copy-start.2 = (bf16[512,2048]{1,0:T(8,128)(2,1)S(1)}, bf16[512,2048]{1,0:T(8,128)(2,1)}, u32[]{:S(2)}) copy-start(bf16[512,2048]{1,0:T(8,128)(2,1)} %g_ref.3) | copy-start | bytes 6291460

commit v2 on v1

v2 whole, which is shorter than its diff:
```python
import functools
import math

import jax
import jax.numpy as jnp
from jax import lax
from jax.experimental import pallas as pl
from jax.experimental.pallas import tpu as pltpu
from jax.sharding import PartitionSpec as P

HD = 128
BLK = 256
SCALE = 1.0 / math.sqrt(HD)
EXP_SCALE = SCALE * math.log2(math.e)
NEG = -1e30
F32 = jnp.float32
BF16 = jnp.bfloat16


def dot_nt(a, b):
    return lax.dot_general(a, b, (((1,), (1,)), ((), ())), preferred_element_type=F32)


def dot_nn(a, b):
    return lax.dot_general(a, b, (((1,), (0,)), ((), ())), preferred_element_type=F32)


def live_rows(block, start, length):
    parts = []
    for at in range(0, block.shape[0], HD):
        factor = (start + at < length).astype(F32).astype(BF16)
        parts.append(block[at : at + HD] * factor)
    return jnp.concatenate(parts, axis=0)


def causal(s):
    key = lax.broadcasted_iota(jnp.int32, s.shape, 0)
    query = lax.broadcasted_iota(jnp.int32, s.shape, 1)
    return jnp.where(key <= query, s, NEG)


def stacked(ref, head):
    return ref[:, head * HD : (head + 1) * HD]


def own_forward(q_ref, k_ref, v_ref, mixed_ref, stats_ref, vt_ref, s_refs, w_refs, *, per_group):
    heads = mixed_ref.shape[0]
    rows = q_ref.shape[0]

    @pl.when(pl.program_id(0) % (per_group // heads) == 0)
    def _():
        vt_ref[...] = v_ref[...].T

    def scores(u):
        q = stacked(q_ref, u)
        for at in range(0, rows, BLK):
            end = at + BLK
            s_refs[u % 2][:end, at:end] = dot_nt(k_ref[:end, :], q[at:end])

    def mix(u):
        s_ref, w_ref = s_refs[u % 2], w_refs[u % 2]
        for at in range(0, rows, BLK):
            end = at + BLK
            tail = causal(s_ref[at:end, at:end])
            peak = jnp.max(tail, axis=0, keepdims=True)
            if at:
                peak = jnp.maximum(peak, jnp.max(s_ref[:at, at:end], axis=0, keepdims=True))
            e = jnp.exp2((tail - peak) * EXP_SCALE)
            total = jnp.sum(e, axis=0, keepdims=True)
            w_ref[at:end, at:end] = e.astype(BF16)
            if at:
                e = jnp.exp2((s_ref[:at, at:end] - peak) * EXP_SCALE)
                total += jnp.sum(e, axis=0, keepdims=True)
                w_ref[:at, at:end] = e.astype(BF16)
            mixed_ref[u, :, at:end] = dot_nn(vt_ref[:, :end], w_ref[:end, at:end])
            stats_ref[u, 0:1, at:end] = peak
            stats_ref[u, 1:2, at:end] = total

    for step in range(heads + 1):
        if step < heads:
            scores(step)
        if step:
            mix(step - 1)


def shared_pass(
    lengths_ref, q_ref, g_ref, near_ref, mixed_ref, stats_ref,
    att_ref, qg_ref, back_ref, terms_ref,
    near_wide, k_ref, v_ref, kt_ref, vt_ref, kg_ref, vg_ref, s_refs, dp_refs, w_refs, ds_refs,
    *, per_group
):
    length = lengths_ref[lax.axis_index("resp")]
    heads = mixed_ref.shape[0]
    rows = q_ref.shape[0]
    groups, near = k_ref.shape[:2]
    senders, chunk = near_ref.shape[:2]
    tokens = near // senders
    steps = per_group // heads
    step_id = pl.program_id(0)
    group = step_id // steps

    @pl.when(step_id == 0)
    def _():
        near_wide[...] = near_ref[...].astype(F32).reshape(senders * chunk, HD)
        for which, (ref, t_ref) in enumerate(((k_ref, kt_ref), (v_ref, vt_ref))):
            for one in range(groups):
                for token in range(tokens):
                    row = (which * groups + one) * tokens + token
                    piece = near_wide[pl.ds(row, senders, stride=chunk), :].astype(BF16)
                    ref[one, token * senders : (token + 1) * senders, :] = piece
                t_ref[one] = ref[one].T

    @pl.when(step_id % steps == 0)
    def _():
        kg_ref[...] = jnp.zeros_like(kg_ref)
        vg_ref[...] = jnp.zeros_like(vg_ref)

    peaks, inverses, drifts, scaled = {}, {}, {}, {}

    def grads(u):
        return live_rows(stacked(g_ref, u), 0, length)

    def scores(u):
        s = dot_nt(k_ref[group], stacked(q_ref, u))
        s_refs[u % 3][...] = s
        peaks[u] = jnp.maximum(jnp.max(s, axis=0, keepdims=True), stats_ref[u, 0:1, :])
        dp_refs[u % 3][...] = dot_nt(v_ref[group], grads(u))

    def mix(u):
        s_ref, w_ref = s_refs[u % 3], w_refs[u % 3]
        e = jnp.exp2((s_ref[...] - peaks[u]) * EXP_SCALE)
        s_ref[...] = e
        decay = jnp.exp2((stats_ref[u, 0:1, :] - peaks[u]) * EXP_SCALE)
        total = jnp.sum(e, axis=0, keepdims=True) + stats_ref[u, 1:2, :] * decay
        inverses[u] = 1.0 / total
        w_ref[...] = (s_ref[...] * inverses[u]).astype(BF16)
        mixed = dot_nn(vt_ref[group], w_ref[...]) + mixed_ref[u] * (decay * inverses[u])
        live = lax.broadcasted_iota(jnp.int32, (1, rows), 1) < length
        att_ref[:, u * HD : (u + 1) * HD] = jnp.where(live, mixed, 0.0).T.astype(BF16)
        drifts[u] = jnp.sum(grads(u).T.astype(F32) * mixed, axis=0, keepdims=True)
        back_ref[u, 0:1, :] = peaks[u]
        back_ref[u, 1:2, :] = inverses[u]
        back_ref[u, 2:3, :] = drifts[u]

    def spread(u):
        s_ref, dp_ref, w_ref, ds_ref = s_refs[u % 3], dp_refs[u % 3], w_refs[u % 3], ds_refs[u % 2]
        ds = s_ref[...] * (dp_ref[...] - drifts[u]) * (inverses[u] * SCALE)
        ds_ref[...] = ds.astype(BF16)
        qg_ref[u] = dot_nn(kt_ref[group], ds_ref[...])
        kg_ref[...] += dot_nn(ds_ref[...], stacked(q_ref, u))
        vg_ref[...] += dot_nn(w_ref[...], grads(u))

    for step in range(heads + 2):
        if step < heads:
            scores(step)
        if 0 <= step - 1 < heads:
            mix(step - 1)
        if step >= 2:
            spread(step - 2)

    for one in range(groups):
        @pl.when(step_id == (one + 1) * steps - 1)
        def _():
            for which, ref in enumerate((kg_ref, vg_ref)):
                for token in range(tokens):
                    row = (which * groups + one) * tokens + token
                    near_wide[pl.ds(row, senders, stride=chunk), :] = ref[
                        token * senders : (token + 1) * senders, :
                    ]

    @pl.when(step_id == groups * steps - 1)
    def _():
        terms_ref[...] = near_wide[...].reshape(senders, chunk, HD).astype(BF16)


def own_backward(
    lengths_ref, q_ref, g_ref, k_ref, v_ref, part_ref, back_ref,
    qg_ref, kg_ref, vg_ref, kt_ref, kacc_ref, vacc_ref, s_refs, dp_refs, w_refs, ds_refs,
    *, per_group
):
    length = lengths_ref[lax.axis_index("resp")]
    heads = part_ref.shape[0]
    rows = q_ref.shape[0]
    steps = per_group // heads
    turn = pl.program_id(0) % steps

    @pl.when(turn == 0)
    def _():
        kt_ref[...] = k_ref[...].T
        kacc_ref[...] = jnp.zeros_like(kacc_ref)
        vacc_ref[...] = jnp.zeros_like(vacc_ref)

    def scores(u):
        q = stacked(q_ref, u)
        g = live_rows(stacked(g_ref, u), 0, length)
        for at in range(0, rows, BLK):
            end = at + BLK
            s_refs[u % 2][:end, at:end] = dot_nt(k_ref[:end, :], q[at:end])
            dp_refs[u % 2][:end, at:end] = dot_nt(v_ref[:end, :], g[at:end])

    def spread(u):
        s_ref, dp_ref, w_ref, ds_ref = (refs[u % 2] for refs in (s_refs, dp_refs, w_refs, ds_refs))
        q = stacked(q_ref, u)
        g = live_rows(stacked(g_ref, u), 0, length)
        for at in range(0, rows, BLK):
            end = at + BLK
            peak = back_ref[u, 0:1, at:end]
            inverse = back_ref[u, 1:2, at:end]
            drift = back_ref[u, 2:3, at:end]
            for low in range(0, end, BLK):
                keys = slice(low, low + BLK)
                s = s_ref[keys, at:end]
                if low == at:
                    s = causal(s)
                p = jnp.exp2((s - peak) * EXP_SCALE) * inverse
                w_ref[keys, at:end] = p.astype(BF16)
                ds_ref[keys, at:end] = (p * (dp_ref[keys, at:end] - drift) * SCALE).astype(BF16)
            qg = dot_nn(kt_ref[:, :end], ds_ref[:end, at:end]) + part_ref[u, :, at:end]
            qg_ref[at:end, u * HD : (u + 1) * HD] = qg.T.astype(BF16)
        for low in range(0, rows, BLK):
            keys = slice(low, low + BLK)
            kacc_ref[keys, :] += dot_nn(ds_ref[keys, low:], q[low:])
            vacc_ref[keys, :] += dot_nn(w_ref[keys, low:], g[low:])

    for step in range(heads + 1):
        if step < heads:
            scores(step)
        if step:
            spread(step - 1)

    @pl.when(turn == steps - 1)
    def _():
        kg_ref[...] = kacc_ref[...].astype(BF16)
        vg_ref[...] = vacc_ref[...].astype(BF16)


def copy_pieces(k_ref, v_ref, out_ref):
    tokens, width = k_ref.shape
    shares, copies = out_ref.shape[:2]
    groups = width // shares // HD
    for share in range(shares):
        parts = []
        for ref in (k_ref, v_ref):
            for one in range(groups):
                at = (share * groups + one) * HD
                parts.append(ref[:, at : at + HD].astype(F32))
        piece = jnp.concatenate(parts, axis=0).astype(BF16)
        out_ref[share] = jnp.broadcast_to(piece[None], (copies,) + piece.shape)


def add_terms(terms_ref, k_ref, v_ref):
    tokens, width = k_ref.shape
    shares = terms_ref.shape[0]
    groups = width // shares // HD
    for share in range(shares):
        total = jnp.sum(terms_ref[share].astype(F32), axis=0)
        for which, ref in enumerate((k_ref, v_ref)):
            for one in range(groups):
                row = (which * groups + one) * tokens
                at = (share * groups + one) * HD
                ref[:, at : at + HD] = total[row : row + tokens].astype(BF16)


VMEM_LIMIT = 60 * 2**20
TURN = 4


def params():
    return pltpu.CompilerParams(
        dimension_semantics=("arbitrary",), vmem_limit_bytes=VMEM_LIMIT
    )


def shape(dims, dtype=F32):
    return jax.ShapeDtypeStruct(dims, dtype)


def specs(rows, per_group):
    steps = per_group // TURN
    return (
        pl.BlockSpec((rows, TURN * HD), lambda h: (0, h)),
        pl.BlockSpec((rows, HD), lambda h: (0, h // steps)),
        pl.BlockSpec((TURN, HD, rows), lambda h: (h, 0, 0)),
        pl.BlockSpec((TURN, 8, rows), lambda h: (h, 0, 0)),
    )


def cost(heads, rows, keys, matmuls, mib):
    return pl.CostEstimate(
        flops=2 * matmuls * heads * rows * keys * HD,
        bytes_accessed=mib * 2**20,
        transcendentals=heads * rows * keys,
    )


def run_own_forward(q, k, v):
    rows, width = q.shape
    heads, groups = width // HD, k.shape[1] // HD
    head, group, wide, stat = specs(rows, heads // groups)
    return pl.pallas_call(
        functools.partial(own_forward, per_group=heads // groups),
        grid=(heads // TURN,),
        in_specs=[head, group, group],
        out_specs=[wide, stat],
        out_shape=[shape((heads, HD, rows)), shape((heads, 8, rows))],
        scratch_shapes=[
            pltpu.VMEM((HD, rows), BF16),
            [pltpu.VMEM((rows, rows), F32)] * 2,
            [pltpu.VMEM((rows, rows), BF16)] * 2,
        ],
        compiler_params=params(),
        cost_estimate=cost(heads, rows, rows, 2, 8),
        name="own_forward",
    )(q, k, v)


def run_shared(lengths, q, g, arrived, mixed, stats):
    rows, width = q.shape
    heads = width // HD
    senders, chunk = arrived.shape[:2]
    groups = 2
    near = senders * chunk // (2 * groups)
    head, _, wide, stat = specs(rows, heads // groups)
    whole = pl.BlockSpec(arrived.shape, lambda h: (0, 0, 0))
    return pl.pallas_call(
        functools.partial(shared_pass, per_group=heads // groups),
        grid=(heads // TURN,),
        in_specs=[pl.BlockSpec(memory_space=pltpu.SMEM), head, head, whole, wide, stat],
        out_specs=[head, wide, stat, whole],
        out_shape=[
            shape((rows, width), BF16), shape((heads, HD, rows)), shape((heads, 8, rows)),
            shape(arrived.shape, BF16),
        ],
        scratch_shapes=[
            pltpu.VMEM((senders * chunk, HD), F32),
            pltpu.VMEM((groups, near, HD), BF16),
            pltpu.VMEM((groups, near, HD), BF16),
            pltpu.VMEM((groups, HD, near), BF16),
            pltpu.VMEM((groups, HD, near), BF16),
            pltpu.VMEM((near, HD), F32),
            pltpu.VMEM((near, HD), F32),
            [pltpu.VMEM((near, rows), F32)] * 3,
            [pltpu.VMEM((near, rows), F32)] * 3,
            [pltpu.VMEM((near, rows), BF16)] * 3,
            [pltpu.VMEM((near, rows), BF16)] * 2,
        ],
        compiler_params=params(),
        cost_estimate=cost(heads, rows, near, 6, 16),
        name="shared_pass",
    )(lengths, q, g, arrived, mixed, stats)


def run_own_backward(lengths, q, g, k, v, part, back):
    rows, width = q.shape
    heads, groups = width // HD, k.shape[1] // HD
    head, group, wide, stat = specs(rows, heads // groups)
    return pl.pallas_call(
        functools.partial(own_backward, per_group=heads // groups),
        grid=(heads // TURN,),
        in_specs=[
            pl.BlockSpec(memory_space=pltpu.SMEM), head, head, group, group, wide, stat
        ],
        out_specs=[head, group, group],
        out_shape=[shape((rows, width), BF16), shape(k.shape, BF16), shape(v.shape, BF16)],
        scratch_shapes=[
            pltpu.VMEM((HD, rows), BF16),
            pltpu.VMEM((rows, HD), F32),
            pltpu.VMEM((rows, HD), F32),
            [pltpu.VMEM((rows, rows), F32)] * 2,
            [pltpu.VMEM((rows, rows), F32)] * 2,
            [pltpu.VMEM((rows, rows), BF16)] * 2,
            [pltpu.VMEM((rows, rows), BF16)] * 2,
        ],
        compiler_params=params(),
        cost_estimate=cost(heads, rows, rows, 5, 12),
        name="own_backward",
    )(lengths, q, g, k, v, part, back)


def on_device(prompt_keys, prompt_values, q, resp_k, resp_v, grad_out, lengths):
    axes = ("prompt", "resp")
    shares = lax.axis_size("prompt")
    copies = lax.axis_size("resp")
    tokens, width = prompt_keys.shape
    chunk = 2 * tokens * width // shares // HD

    pieces = pl.pallas_call(
        copy_pieces,
        out_shape=shape((shares, copies, chunk, HD), BF16),
        compiler_params=pltpu.CompilerParams(vmem_limit_bytes=VMEM_LIMIT),
        name="copy_pieces",
    )(prompt_keys, prompt_values)
    pieces = pieces.reshape(shares * copies, chunk, HD)
    arrived = lax.all_to_all(pieces, axes, split_axis=0, concat_axis=0, tiled=True)

    mixed, stats = run_own_forward(q, resp_k, resp_v)
    attended, part, back, terms = run_shared(lengths, q, grad_out, arrived, mixed, stats)
    terms = lax.all_to_all(terms, axes, split_axis=0, concat_axis=0, tiled=True)
    query_grads, key_grads, value_grads = run_own_backward(
        lengths, q, grad_out, resp_k, resp_v, part, back
    )
    prompt_kg, prompt_vg = pl.pallas_call(
        add_terms,
        out_shape=[shape((tokens, width), BF16)] * 2,
        compiler_params=pltpu.CompilerParams(vmem_limit_bytes=VMEM_LIMIT),
        name="add_terms",
    )(terms.reshape(shares, copies, chunk, HD))
    return attended, query_grads, key_grads, value_grads, prompt_kg, prompt_vg


def solution(mesh):
    return jax.shard_map(
        on_device,
        mesh=mesh,
        in_specs=(
            P(("prompt", "resp"), None),
            P(("prompt", "resp"), None),
            P("resp", "prompt"),
            P("resp", "prompt"),
            P("resp", "prompt"),
            P("resp", "prompt"),
            P(),
        ),
        out_specs=(
            P("resp", "prompt"),
            P("resp", "prompt"),
            P("resp", "prompt"),
            P("resp", "prompt"),
            P(("prompt", "resp"), None),
            P(("prompt", "resp"), None),
        ),
        check_vma=False,
    )
```

time: 106 us -> 70.3 us (0.66)
  Pallas kernels: 69.8 us -> 43.5 us
  local copies, waits for them, and re-layouts: 13 us -> 1.59 us
  waiting for transfers between devices: 0.01 us -> 8.16 us
  starting transfers between devices: 21.3 us -> 16.1 us
    pallas_call x3 -> x5, Pallas kernels: 69.8 us -> 43.5 us  [the longest x1 21 us: run_shared(): pl.pallas_call(functools.partial(shared_pass, per_group=heads // groups),...]
    all_to_all x1, waiting for transfers between devices: 0.01 us -> 5.95 us  [on_device(): lax.all_to_all(pieces, axes, split_axis=0, concat_axis=0, tiled=True)]
    all_to_all x1, starting transfers between devices: 9.76 us -> 4.6 us  [on_device(): terms = lax.all_to_all(terms, axes, split_axis=0, concat_axis=0, tiled=True)]
    unnamed x14 -> x4, local copies, waits for them, and re-layouts: 6.55 us -> 1.59 us
    all_to_all x1, waiting for transfers between devices: 0.01 us -> 2.2 us  [on_device(): terms = lax.all_to_all(terms, axes, split_axis=0, concat_axis=0, tiled=True)]
    another operation x2 -> x0, local copies, waits for them, and re-layouts: 1.42 us -> none  [on_device(): pieces = jnp.stack([prompt_keys, prompt_values], axis=1)]
    convert_element_type x1 -> x0, local copies, waits for them, and re-layouts: 1.34 us -> none  [on_device(): terms = jnp.stack([kg, vg]).transpose(2, 0, 1, 3).astype(BF16)]
    squeeze x3 -> x0, local copies, waits for them, and re-layouts: 1.25 us -> none  [the longest x2 1.22 us: on_device(): return (attended, query_grads, key_grads, value_grads, sums[0], sums[1])]
  transfers between devices with their start and end apart: 2 -> 2, of which waited for: 0 -> 2; matrix products, arithmetic and copies ran while one was open for 1% -> 0% of each run, Pallas kernels for 33% -> 27%
where the time goes in v2:
time: 70.3 us; the launch traced here: 70 us
  Pallas kernels  43.5 us (62%)
  starting transfers between devices  16.1 us (23%)
  waiting for transfers between devices  8.16 us (12%)
  local copies, waits for them, and re-layouts  1.59 us (2%)
    pallas_call x1, Pallas kernels, run_shared(): pl.pallas_call(functools.partial(shared_pass, per_group=heads // groups),...  21 us
    pallas_call x1, Pallas kernels, run_own_backward(): pl.pallas_call(functools.partial(own_backward, per_group=heads // groups)...  11.5 us
    all_to_all x1, starting transfers between devices, on_device(): lax.all_to_all(pieces, axes, split_axis=0, concat_axis=0, tiled=True)  11.5 us
    pallas_call x1, Pallas kernels, run_own_forward(): pl.pallas_call(functools.partial(own_forward, per_group=heads // groups),...  7.65 us
    all_to_all x1, waiting for transfers between devices, on_device(): lax.all_to_all(pieces, axes, split_axis=0, concat_axis=0, tiled=True)  5.95 us
    all_to_all x1, starting transfers between devices, on_device(): terms = lax.all_to_all(terms, axes, split_axis=0, concat_axis=0, tiled=True)  4.6 us
    all_to_all x1, waiting for transfers between devices, on_device(): terms = lax.all_to_all(terms, axes, split_axis=0, concat_axis=0, tiled=True)  2.2 us
    pallas_call x1, Pallas kernels, on_device(): pl.pallas_call(add_terms, out_shape=[shape((tokens, width), BF16)] * 2, c...  1.73 us
  transfers between devices with their start and end apart: 2, of which 2 were waited for; matrix products, arithmetic and copies ran while one was open for 0% of the time, Pallas kernels for 27%

profile of v2, /device:TPU:1, one launch (start us, length us, event | category | flops | bytes accessed | tf_op | source)
XLA Modules:
  0.0 70.0 jit_solution(14804240201612435353)
XLA Ops:
  0.6 1.5 %copy_pieces.1 = bf16[4,32,16,128]{3,2,1,0:T(8,128)(2,1)} custom-call(bf16[4,1024]{1,0:T(4,128)(2,1)} %k_ref.3, bf16[4,1024]{1,0:T(4,128)(2,1)} %v_ref.3), custom_call_target="tpu_custom_call" | custom-call | tf_op jit(solution)/shard_map/copy_pieces/pallas_call | solution.py:387
  2.2 11.5 %all-to-all-start = ((bf16[128,16,128]{2,1,0:T(8,128)(2,1)}), bf16[128,16,128]{2,1,0:T(8,128)(2,1)S(1)}, u32[]{:S(2)}, u32[]{:S(2)}) async-start(bf16[128,16,128]{2,1,0:T(8,128)(2,1)} %bitcast.3), calls=%async_computation | async-start | bytes 1048576 | tf_op jit(solution)/shard_map/all_to_all | solution.py:394
  13.7 7.6 %own_forward.1 = (f32[16,128,512]{2,1,0:T(8,128)}, f32[16,8,512]{2,1,0:T(8,128)}) custom-call(bf16[512,2048]{1,0:T(8,128)(2,1)} %q_ref.5, bf16[512,256]{1,0:T(8,128)(2,1)} %k_ref.5, bf16[512,256]{1,0:T(8,128)(2,1)} %v_ref.5), custom_call_target="tpu_custom_call" | custom-call | flops 2147483648 | bytes 8388608 | tf_op jit(solution)/shard_map/own_forward/pallas_call | solution.py:300
  21.3 6.0 %all-to-all-done.near_ref = bf16[128,16,128]{2,1,0:T(8,128)(2,1)S(1)} async-done(((bf16[128,16,128]{2,1,0:T(8,128)(2,1)}), bf16[128,16,128]{2,1,0:T(8,128)(2,1)S(1)}, u32[]{:S(2)}, u32[]{:S(2)}) %all-to-all-start) | async-done | bytes 524320 | tf_op jit(solution)/shard_map/all_to_all | solution.py:394
  27.3 0.0 copy-start.1
  27.3 0.8 %copy-done.1 = bf16[128,16,128]{2,1,0:T(8,128)(2,1)} copy-done((bf16[128,16,128]{2,1,0:T(8,128)(2,1)}, bf16[128,16,128]{2,1,0:T(8,128)(2,1)S(1)}, u32[]{:S(2)}) %copy-start.1) | copy-done | bytes 524312
  28.1 21.0 %shared_pass.1 = (bf16[512,2048]{1,0:T(8,128)(2,1)}, f32[16,128,512]{2,1,0:T(8,128)}, f32[16,8,512]{2,1,0:T(8,128)}, bf16[128,16,128]{2,1,0:T(8,128)(2,1)}) custom-call(s32[32]{0:T(128)} %lengths_ref.3, bf16[512,2048]{1,0:T(8,128)(2,1)} %q_ref.5, bf16[512,2048]{1,0:T(8,128)(2,1)} %g_ref.3, bf16[128,16,128]{2,1,0:T(8,128)(2,1)} %copy-done.1, ...), custom_call_target="tpu_custom_call" | custom-call | flops 6442450944 | bytes 16777216 | tf_op jit(solution)/shard_map/shared_pass/pallas_call | solution.py:325
  49.1 4.6 %all-to-all-start.1 = ((bf16[128,16,128]{2,1,0:T(8,128)(2,1)}), bf16[128,16,128]{2,1,0:T(8,128)(2,1)S(1)}, u32[]{:S(2)}, u32[]{:S(2)}) async-start(bf16[128,16,128]{2,1,0:T(8,128)(2,1)} %get-tuple-element.25), calls=%async_computation.1 | async-start | bytes 1048576 | tf_op jit(solution)/shard_map/all_to_all | solution.py:398
  53.7 11.5 %own_backward.1 = (bf16[512,2048]{1,0:T(8,128)(2,1)}, bf16[512,256]{1,0:T(8,128)(2,1)}, bf16[512,256]{1,0:T(8,128)(2,1)}) custom-call(s32[32]{0:T(128)} %lengths_ref.3, bf16[512,2048]{1,0:T(8,128)(2,1)} %q_ref.5, bf16[512,2048]{1,0:T(8,128)(2,1)} %g_ref.3, bf16[512,256]{1,0:T(8,128)(2,1)} %k_ref.5, bf16[512,256]{1,0:T(8,128)(2,1)} %v_ref.5, ...), custom_call_target="tpu_custom_call" | custom-call | flops 5368709120 | bytes 12582912 | tf_op jit(solution)/shard_map/own_backward/pallas_call | solution.py:357
  65.2 2.2 %all-to-all-done.1 = bf16[128,16,128]{2,1,0:T(8,128)(2,1)S(1)} async-done(((bf16[128,16,128]{2,1,0:T(8,128)(2,1)}), bf16[128,16,128]{2,1,0:T(8,128)(2,1)S(1)}, u32[]{:S(2)}, u32[]{:S(2)}) %all-to-all-start.1) | async-done | bytes 524320 | tf_op jit(solution)/shard_map/all_to_all | solution.py:398
  67.4 0.0 copy-start
  67.4 0.8 %copy-done = bf16[128,16,128]{2,1,0:T(8,128)(2,1)} copy-done((bf16[128,16,128]{2,1,0:T(8,128)(2,1)}, bf16[128,16,128]{2,1,0:T(8,128)(2,1)S(1)}, u32[]{:S(2)}) %copy-start) | copy-done | bytes 524312
  68.2 1.7 %add_terms.1 = (bf16[4,1024]{1,0:T(4,128)(2,1)}, bf16[4,1024]{1,0:T(4,128)(2,1)}) custom-call(bf16[4,32,16,128]{3,2,1,0:T(8,128)(2,1)} %bitcast.2), custom_call_target="tpu_custom_call" | custom-call | tf_op jit(solution)/shard_map/add_terms/pallas_call | solution.py:402
Async XLA Ops:
  2.2 25.1 %all-to-all-start = ((bf16[128,16,128]{2,1,0:T(8,128)(2,1)}), bf16[128,16,128]{2,1,0:T(8,128)(2,1)S(1)}, u32[]{:S(2)}, u32[]{:S(2)}) async-start(bf16[128,16,128]{2,1,0:T(8,128)(2,1)} %bitcast.3), calls=%async_computation | async-start | bytes 1048576 | tf_op jit(solution)/shard_map/all_to_all | solution.py:394
  27.3 0.8 %copy-start.1 = (bf16[128,16,128]{2,1,0:T(8,128)(2,1)}, bf16[128,16,128]{2,1,0:T(8,128)(2,1)S(1)}, u32[]{:S(2)}) copy-start(bf16[128,16,128]{2,1,0:T(8,128)(2,1)S(1)} %all-to-all-done.near_ref) | copy-start | bytes 1572868
  49.1 18.3 %all-to-all-start.1 = ((bf16[128,16,128]{2,1,0:T(8,128)(2,1)}), bf16[128,16,128]{2,1,0:T(8,128)(2,1)S(1)}, u32[]{:S(2)}, u32[]{:S(2)}) async-start(bf16[128,16,128]{2,1,0:T(8,128)(2,1)} %get-tuple-element.25), calls=%async_computation.1 | async-start | bytes 1048576 | tf_op jit(solution)/shard_map/all_to_all | solution.py:398
  67.4 0.8 %copy-start = (bf16[128,16,128]{2,1,0:T(8,128)(2,1)}, bf16[128,16,128]{2,1,0:T(8,128)(2,1)S(1)}, u32[]{:S(2)}) copy-start(bf16[128,16,128]{2,1,0:T(8,128)(2,1)S(1)} %all-to-all-done.1) | copy-start | bytes 1572868

commit v3 on v2

--- a/solution.py
+++ b/solution.py
@@ -261,7 +261,7 @@
                 ref[:, at : at + HD] = total[row : row + tokens].astype(BF16)
 
 
-VMEM_LIMIT = 60 * 2**20
+VMEM_LIMIT = 40 * 2**20
 TURN = 4
 
 
@@ -273,6 +273,14 @@
 
 def shape(dims, dtype=F32):
     return jax.ShapeDtypeStruct(dims, dtype)
+
+
+def hbm_shape(dims, dtype=F32):
+    return pltpu.HBM(dims, dtype)
+
+
+def in_hbm(*arrays):
+    return tuple(pltpu.with_memory_space_constraint(a, pltpu.HBM) for a in arrays)
 
 
 def specs(rows, per_group):
@@ -302,7 +310,7 @@
         grid=(heads // TURN,),
         in_specs=[head, group, group],
         out_specs=[wide, stat],
-        out_shape=[shape((heads, HD, rows)), shape((heads, 8, rows))],
+        out_shape=[hbm_shape((heads, HD, rows)), hbm_shape((heads, 8, rows))],
         scratch_shapes=[
             pltpu.VMEM((HD, rows), BF16),
             [pltpu.VMEM((rows, rows), F32)] * 2,
@@ -328,8 +336,8 @@
         in_specs=[pl.BlockSpec(memory_space=pltpu.SMEM), head, head, whole, wide, stat],
         out_specs=[head, wide, stat, whole],
         out_shape=[
-            shape((rows, width), BF16), shape((heads, HD, rows)), shape((heads, 8, rows)),
-            shape(arrived.shape, BF16),
+            hbm_shape((rows, width), BF16), hbm_shape((heads, HD, rows)),
+            hbm_shape((heads, 8, rows)), hbm_shape(arrived.shape, BF16),
         ],
         scratch_shapes=[
             pltpu.VMEM((senders * chunk, HD), F32),
@@ -384,6 +392,7 @@
     tokens, width = prompt_keys.shape
     chunk = 2 * tokens * width // shares // HD
 
+    prompt_keys, prompt_values = in_hbm(prompt_keys, prompt_values)
     pieces = pl.pallas_call(
         copy_pieces,
         out_shape=shape((shares, copies, chunk, HD), BF16),
@@ -393,8 +402,10 @@
     pieces = pieces.reshape(shares * copies, chunk, HD)
     arrived = lax.all_to_all(pieces, axes, split_axis=0, concat_axis=0, tiled=True)
 
-    mixed, stats = run_own_forward(q, resp_k, resp_v)
+    q, resp_k, resp_v, grad_out = in_hbm(q, resp_k, resp_v, grad_out)
+    mixed, stats = in_hbm(*run_own_forward(q, resp_k, resp_v))
     attended, part, back, terms = run_shared(lengths, q, grad_out, arrived, mixed, stats)
+    part, back = in_hbm(part, back)
     terms = lax.all_to_all(terms, axes, split_axis=0, concat_axis=0, tiled=True)
     query_grads, key_grads, value_grads = run_own_backward(
         lengths, q, grad_out, resp_k, resp_v, part, back

time: 70.3 us -> 67.4 us (0.959)
  local copies, waits for them, and re-layouts: 1.59 us -> 0.01 us
  Pallas kernels: 43.5 us -> 42.1 us
    unnamed x4 -> x2, local copies, waits for them, and re-layouts: 1.59 us -> 0.01 us
    pallas_call x1, Pallas kernels: 1.73 us -> 0.69 us  [on_device(): pl.pallas_call(add_terms, out_shape=[shape((tokens, width), BF16)] * 2, c...]
  transfers between devices with their start and end apart: 2 -> 2, of which waited for: 2 -> 2; matrix products, arithmetic and copies ran while one was open for 0% -> 0% of each run, Pallas kernels for 27% -> 29%
where the time goes in v3:
time: 67.4 us; the launch traced here: 67 us
  Pallas kernels  42.1 us (62%)
  starting transfers between devices  16.1 us (24%)
  waiting for transfers between devices  8.16 us (12%)
    pallas_call x1, Pallas kernels, run_shared(): pl.pallas_call(functools.partial(shared_pass, per_group=heads // groups),...  20.7 us
    pallas_call x1, Pallas kernels, run_own_backward(): pl.pallas_call(functools.partial(own_backward, per_group=heads // groups)...  11.5 us
    all_to_all x1, starting transfers between devices, on_device(): lax.all_to_all(pieces, axes, split_axis=0, concat_axis=0, tiled=True)  11.5 us
    pallas_call x1, Pallas kernels, run_own_forward(): pl.pallas_call(functools.partial(own_forward, per_group=heads // groups),...  7.65 us
    all_to_all x1, waiting for transfers between devices, on_device(): lax.all_to_all(pieces, axes, split_axis=0, concat_axis=0, tiled=True)  5.94 us
    all_to_all x1, starting transfers between devices, on_device(): terms = lax.all_to_all(terms, axes, split_axis=0, concat_axis=0, tiled=True)  4.59 us
    all_to_all x1, waiting for transfers between devices, on_device(): terms = lax.all_to_all(terms, axes, split_axis=0, concat_axis=0, tiled=True)  2.22 us
    pallas_call x1, Pallas kernels, on_device(): pl.pallas_call(copy_pieces, out_shape=shape((shares, copies, chunk, HD),...  1.55 us
  transfers between devices with their start and end apart: 2, of which 2 were waited for; matrix products, arithmetic and copies ran while one was open for 0% of the time, Pallas kernels for 29%

profile of v3, /device:TPU:1, one launch (start us, length us, event | category | flops | bytes accessed | tf_op | source)
XLA Modules:
  0.0 67.0 jit_solution(5343142120357024639)
XLA Ops:
  0.6 1.5 %copy_pieces.1 = bf16[4,32,16,128]{3,2,1,0:T(8,128)(2,1)} custom-call(bf16[4,1024]{1,0:T(4,128)(2,1)} %k_ref.3, bf16[4,1024]{1,0:T(4,128)(2,1)} %v_ref.3), custom_call_target="tpu_custom_call" | custom-call | tf_op jit(solution)/shard_map/copy_pieces/pallas_call | solution.py:396
  2.2 11.5 %all-to-all-start = ((bf16[128,16,128]{2,1,0:T(8,128)(2,1)}), bf16[128,16,128]{2,1,0:T(8,128)(2,1)S(1)}, u32[]{:S(2)}, u32[]{:S(2)}) async-start(bf16[128,16,128]{2,1,0:T(8,128)(2,1)} %bitcast), calls=%async_computation | async-start | bytes 1048576 | tf_op jit(solution)/shard_map/all_to_all | solution.py:403
  13.7 0.0 copy-start
  13.7 7.6 %own_forward.1 = (f32[16,128,512]{2,1,0:T(8,128)}, f32[16,8,512]{2,1,0:T(8,128)}) custom-call(bf16[512,2048]{1,0:T(8,128)(2,1)} %q_ref.5, bf16[512,256]{1,0:T(8,128)(2,1)} %k_ref.5, bf16[512,256]{1,0:T(8,128)(2,1)} %v_ref.5), custom_call_target="tpu_custom_call" | custom-call | flops 2147483648 | bytes 8388608 | tf_op jit(solution)/shard_map/own_forward/pallas_call | solution.py:308
  21.3 5.9 %all-to-all-done.near_ref = bf16[128,16,128]{2,1,0:T(8,128)(2,1)S(1)} async-done(((bf16[128,16,128]{2,1,0:T(8,128)(2,1)}), bf16[128,16,128]{2,1,0:T(8,128)(2,1)S(1)}, u32[]{:S(2)}, u32[]{:S(2)}) %all-to-all-start) | async-done | bytes 524320 | tf_op jit(solution)/shard_map/all_to_all | solution.py:403
  27.3 0.0 copy-done
  27.3 20.7 %shared_pass.1 = (bf16[512,2048]{1,0:T(8,128)(2,1)}, f32[16,128,512]{2,1,0:T(8,128)}, f32[16,8,512]{2,1,0:T(8,128)}, bf16[128,16,128]{2,1,0:T(8,128)(2,1)}) custom-call(s32[32]{0:T(128)S(1)} %copy-done, bf16[512,2048]{1,0:T(8,128)(2,1)} %q_ref.5, bf16[512,2048]{1,0:T(8,128)(2,1)} %g_ref.3, bf16[128,16,128]{2,1,0:T(8,128)(2,1)S(1)} %all-to-all-done.near_ref, ...), custom_call_target="tpu_custom_call" | custom-call | flops 6442450944 | bytes 16777216 | tf_op jit(solution)/shard_map/shared_pass/pallas_call | solution.py:333
  48.0 4.6 %all-to-all-start.1 = ((bf16[128,16,128]{2,1,0:T(8,128)(2,1)}), bf16[128,16,128]{2,1,0:T(8,128)(2,1)S(1)}, u32[]{:S(2)}, u32[]{:S(2)}) async-start(bf16[128,16,128]{2,1,0:T(8,128)(2,1)} %get-tuple-element.25), calls=%async_computation.1 | async-start | bytes 1048576 | tf_op jit(solution)/shard_map/all_to_all | solution.py:409
  52.6 11.5 %own_backward.1 = (bf16[512,2048]{1,0:T(8,128)(2,1)}, bf16[512,256]{1,0:T(8,128)(2,1)}, bf16[512,256]{1,0:T(8,128)(2,1)}) custom-call(s32[32]{0:T(128)S(1)} %copy-done, bf16[512,2048]{1,0:T(8,128)(2,1)} %q_ref.5, bf16[512,2048]{1,0:T(8,128)(2,1)} %g_ref.3, bf16[512,256]{1,0:T(8,128)(2,1)} %k_ref.5, bf16[512,256]{1,0:T(8,128)(2,1)} %v_ref.5, ...), custom_call_target="tpu_custom_call" | custom-call | flops 5368709120 | bytes 12582912 | tf_op jit(solution)/shard_map/own_backward/pallas_call | solution.py:365
  64.1 2.2 %all-to-all-done.1 = bf16[128,16,128]{2,1,0:T(8,128)(2,1)S(1)} async-done(((bf16[128,16,128]{2,1,0:T(8,128)(2,1)}), bf16[128,16,128]{2,1,0:T(8,128)(2,1)S(1)}, u32[]{:S(2)}, u32[]{:S(2)}) %all-to-all-start.1) | async-done | bytes 524320 | tf_op jit(solution)/shard_map/all_to_all | solution.py:409
  66.3 0.7 %add_terms.1 = (bf16[4,1024]{1,0:T(4,128)(2,1)}, bf16[4,1024]{1,0:T(4,128)(2,1)}) custom-call(bf16[4,32,16,128]{3,2,1,0:T(8,128)(2,1)S(1)} %bitcast.2), custom_call_target="tpu_custom_call" | custom-call | tf_op jit(solution)/shard_map/add_terms/pallas_call | solution.py:413
Async XLA Ops:
  2.2 25.1 %all-to-all-start = ((bf16[128,16,128]{2,1,0:T(8,128)(2,1)}), bf16[128,16,128]{2,1,0:T(8,128)(2,1)S(1)}, u32[]{:S(2)}, u32[]{:S(2)}) async-start(bf16[128,16,128]{2,1,0:T(8,128)(2,1)} %bitcast), calls=%async_computation | async-start | bytes 1048576 | tf_op jit(solution)/shard_map/all_to_all | solution.py:403
  13.7 13.6 %copy-start = (s32[32]{0:T(128)S(1)}, s32[32]{0:T(128)}, u32[]{:S(2)}) copy-start(s32[32]{0:T(128)} %lengths_ref.3) | copy-start | bytes 388
  48.0 18.3 %all-to-all-start.1 = ((bf16[128,16,128]{2,1,0:T(8,128)(2,1)}), bf16[128,16,128]{2,1,0:T(8,128)(2,1)S(1)}, u32[]{:S(2)}, u32[]{:S(2)}) async-start(bf16[128,16,128]{2,1,0:T(8,128)(2,1)} %get-tuple-element.25), calls=%async_computation.1 | async-start | bytes 1048576 | tf_op jit(solution)/shard_map/all_to_all | solution.py:409

commit v4 on v3

--- a/solution.py
+++ b/solution.py
@@ -13,6 +13,8 @@
 SCALE = 1.0 / math.sqrt(HD)
 EXP_SCALE = SCALE * math.log2(math.e)
 NEG = -1e30
+REACH = 100 / EXP_SCALE
+SLACK = 1.02
 F32 = jnp.float32
 BF16 = jnp.bfloat16
 
@@ -43,19 +45,27 @@
     return ref[:, head * HD : (head + 1) * HD]
 
 
-def own_forward(q_ref, k_ref, v_ref, mixed_ref, stats_ref, vt_ref, s_refs, w_refs, *, per_group):
+def own_forward(
+    q_ref, k_ref, v_ref, mixed_ref, stats_ref, limit_ref, vt_ref, s_refs, w_refs, *, per_group
+):
     heads = mixed_ref.shape[0]
     rows = q_ref.shape[0]
 
     @pl.when(pl.program_id(0) % (per_group // heads) == 0)
     def _():
         vt_ref[...] = v_ref[...].T
+
+    @pl.when(pl.program_id(0) == 0)
+    def _():
+        limit_ref[...] = jnp.full(limit_ref.shape, NEG, F32)
 
     def scores(u):
         q = stacked(q_ref, u)
         for at in range(0, rows, BLK):
             end = at + BLK
             s_refs[u % 2][:end, at:end] = dot_nt(k_ref[:end, :], q[at:end])
+        square = dot_nt(jnp.ones((8, HD), BF16), q * q)
+        limit_ref[0:8, :] = jnp.maximum(limit_ref[0:8, :], square)
 
     def mix(u):
         s_ref, w_ref = s_refs[u % 2], w_refs[u % 2]
@@ -75,6 +85,7 @@
             mixed_ref[u, :, at:end] = dot_nn(vt_ref[:, :end], w_ref[:end, at:end])
             stats_ref[u, 0:1, at:end] = peak
             stats_ref[u, 1:2, at:end] = total
+            limit_ref[8:9, at:end] = jnp.maximum(limit_ref[8:9, at:end], -peak)
 
     for step in range(heads + 1):
         if step < heads:
@@ -84,9 +95,10 @@
 
 
 def shared_pass(
-    lengths_ref, q_ref, g_ref, near_ref, mixed_ref, stats_ref,
+    lengths_ref, q_ref, g_ref, near_ref, mixed_ref, stats_ref, limit_ref,
     att_ref, qg_ref, back_ref, terms_ref,
     near_wide, k_ref, v_ref, kt_ref, vt_ref, kg_ref, vg_ref, s_refs, dp_refs, w_refs, ds_refs,
+    peak_ref, close_ref,
     *, per_group
 ):
     length = lengths_ref[lax.axis_index("resp")]
@@ -109,28 +121,42 @@
                     piece = near_wide[pl.ds(row, senders, stride=chunk), :].astype(BF16)
                     ref[one, token * senders : (token + 1) * senders, :] = piece
                 t_ref[one] = ref[one].T
+        wide = kt_ref[...].astype(F32)
+        longest = jnp.sqrt(jnp.max(jnp.sum(wide * wide, axis=1)) * jnp.max(limit_ref[0:8, :]))
+        close_ref[0] = (longest * SLACK + jnp.max(limit_ref[8:9, :]) < REACH).astype(jnp.int32)
 
     @pl.when(step_id % steps == 0)
     def _():
         kg_ref[...] = jnp.zeros_like(kg_ref)
         vg_ref[...] = jnp.zeros_like(vg_ref)
 
-    peaks, inverses, drifts, scaled = {}, {}, {}, {}
+    @pl.when(close_ref[0] != 0)
+    def _():
+        for u in range(heads):
+            peak_ref[u, 0:1, :] = stats_ref[u, 0:1, :]
+
+    @pl.when(close_ref[0] == 0)
+    def _():
+        for u in range(heads):
+            s = dot_nt(k_ref[group], stacked(q_ref, u))
+            peak = jnp.max(s, axis=0, keepdims=True)
+            peak_ref[u, 0:1, :] = jnp.maximum(peak, stats_ref[u, 0:1, :])
+
+    inverses, drifts = {}, {}
 
     def grads(u):
         return live_rows(stacked(g_ref, u), 0, length)
 
     def scores(u):
-        s = dot_nt(k_ref[group], stacked(q_ref, u))
-        s_refs[u % 3][...] = s
-        peaks[u] = jnp.maximum(jnp.max(s, axis=0, keepdims=True), stats_ref[u, 0:1, :])
+        s_refs[u % 3][...] = dot_nt(k_ref[group], stacked(q_ref, u))
         dp_refs[u % 3][...] = dot_nt(v_ref[group], grads(u))
 
     def mix(u):
         s_ref, w_ref = s_refs[u % 3], w_refs[u % 3]
-        e = jnp.exp2((s_ref[...] - peaks[u]) * EXP_SCALE)
+        peak = peak_ref[u, 0:1, :]
+        e = jnp.exp2((s_ref[...] - peak) * EXP_SCALE)
         s_ref[...] = e
-        decay = jnp.exp2((stats_ref[u, 0:1, :] - peaks[u]) * EXP_SCALE)
+        decay = jnp.exp2((stats_ref[u, 0:1, :] - peak) * EXP_SCALE)
         total = jnp.sum(e, axis=0, keepdims=True) + stats_ref[u, 1:2, :] * decay
         inverses[u] = 1.0 / total
         w_ref[...] = (s_ref[...] * inverses[u]).astype(BF16)
@@ -138,7 +164,7 @@
         live = lax.broadcasted_iota(jnp.int32, (1, rows), 1) < length
         att_ref[:, u * HD : (u + 1) * HD] = jnp.where(live, mixed, 0.0).T.astype(BF16)
         drifts[u] = jnp.sum(grads(u).T.astype(F32) * mixed, axis=0, keepdims=True)
-        back_ref[u, 0:1, :] = peaks[u]
+        back_ref[u, 0:1, :] = peak
         back_ref[u, 1:2, :] = inverses[u]
         back_ref[u, 2:3, :] = drifts[u]
 
@@ -309,8 +335,10 @@
         functools.partial(own_forward, per_group=heads // groups),
         grid=(heads // TURN,),
         in_specs=[head, group, group],
-        out_specs=[wide, stat],
-        out_shape=[hbm_shape((heads, HD, rows)), hbm_shape((heads, 8, rows))],
+        out_specs=[wide, stat, pl.BlockSpec((16, rows), lambda h: (0, 0))],
+        out_shape=[
+            hbm_shape((heads, HD, rows)), hbm_shape((heads, 8, rows)), hbm_shape((16, rows)),
+        ],
         scratch_shapes=[
             pltpu.VMEM((HD, rows), BF16),
             [pltpu.VMEM((rows, rows), F32)] * 2,
@@ -322,7 +350,7 @@
     )(q, k, v)
 
 
-def run_shared(lengths, q, g, arrived, mixed, stats):
+def run_shared(lengths, q, g, arrived, mixed, stats, limit):
     rows, width = q.shape
     heads = width // HD
     senders, chunk = arrived.shape[:2]
@@ -333,7 +361,10 @@
     return pl.pallas_call(
         functools.partial(shared_pass, per_group=heads // groups),
         grid=(heads // TURN,),
-        in_specs=[pl.BlockSpec(memory_space=pltpu.SMEM), head, head, whole, wide, stat],
+        in_specs=[
+            pl.BlockSpec(memory_space=pltpu.SMEM), head, head, whole, wide, stat,
+            pl.BlockSpec((16, rows), lambda h: (0, 0)),
+        ],
         out_specs=[head, wide, stat, whole],
         out_shape=[
             hbm_shape((rows, width), BF16), hbm_shape((heads, HD, rows)),
@@ -351,11 +382,13 @@
             [pltpu.VMEM((near, rows), F32)] * 3,
             [pltpu.VMEM((near, rows), BF16)] * 3,
             [pltpu.VMEM((near, rows), BF16)] * 2,
+            pltpu.VMEM((TURN, 8, rows), F32),
+            pltpu.SMEM((1,), jnp.int32),
         ],
         compiler_params=params(),
         cost_estimate=cost(heads, rows, near, 6, 16),
         name="shared_pass",
-    )(lengths, q, g, arrived, mixed, stats)
+    )(lengths, q, g, arrived, mixed, stats, limit)
 
 
 def run_own_backward(lengths, q, g, k, v, part, back):
@@ -403,8 +436,10 @@
     arrived = lax.all_to_all(pieces, axes, split_axis=0, concat_axis=0, tiled=True)
 
     q, resp_k, resp_v, grad_out = in_hbm(q, resp_k, resp_v, grad_out)
-    mixed, stats = in_hbm(*run_own_forward(q, resp_k, resp_v))
-    attended, part, back, terms = run_shared(lengths, q, grad_out, arrived, mixed, stats)
+    mixed, stats, limit = in_hbm(*run_own_forward(q, resp_k, resp_v))
+    attended, part, back, terms = run_shared(
+        lengths, q, grad_out, arrived, mixed, stats, limit
+    )
     part, back = in_hbm(part, back)
     terms = lax.all_to_all(terms, axes, split_axis=0, concat_axis=0, tiled=True)
     query_grads, key_grads, value_grads = run_own_backward(

time: 67.4 us -> 69 us (1.024)
  Pallas kernels: 42.1 us -> 43.9 us
    pallas_call x1, Pallas kernels: 20.7 us -> 22.4 us  [run_shared(): pl.pallas_call(functools.partial(shared_pass, per_group=heads // groups),...]
  transfers between devices with their start and end apart: 2 -> 2, of which waited for: 2 -> 2; matrix products, arithmetic and copies ran while one was open for 0% -> 0% of each run, Pallas kernels for 29% -> 28%
where the time goes in v4:
time: 69 us; the launch traced here: 68.7 us
  Pallas kernels  43.9 us (64%)
  starting transfers between devices  16.1 us (23%)
  waiting for transfers between devices  8.03 us (12%)
    pallas_call x1, Pallas kernels, run_shared(): pl.pallas_call(functools.partial(shared_pass, per_group=heads // groups),...  22.4 us
    pallas_call x1, Pallas kernels, run_own_backward(): pl.pallas_call(functools.partial(own_backward, per_group=heads // groups)...  11.5 us
    all_to_all x1, starting transfers between devices, on_device(): lax.all_to_all(pieces, axes, split_axis=0, concat_axis=0, tiled=True)  11.5 us
    pallas_call x1, Pallas kernels, run_own_forward(): pl.pallas_call(functools.partial(own_forward, per_group=heads // groups),...  7.76 us
    all_to_all x1, waiting for transfers between devices, on_device(): lax.all_to_all(pieces, axes, split_axis=0, concat_axis=0, tiled=True)  5.82 us
    all_to_all x1, starting transfers between devices, on_device(): terms = lax.all_to_all(terms, axes, split_axis=0, concat_axis=0, tiled=True)  4.59 us
    all_to_all x1, waiting for transfers between devices, on_device(): terms = lax.all_to_all(terms, axes, split_axis=0, concat_axis=0, tiled=True)  2.21 us
    pallas_call x1, Pallas kernels, on_device(): pl.pallas_call(copy_pieces, out_shape=shape((shares, copies, chunk, HD),...  1.55 us
  transfers between devices with their start and end apart: 2, of which 2 were waited for; matrix products, arithmetic and copies ran while one was open for 0% of the time, Pallas kernels for 28%

profile of v4, /device:TPU:1, one launch (start us, length us, event | category | flops | bytes accessed | tf_op | source)
XLA Modules:
  0.0 68.7 jit_solution(13360341546183441516)
XLA Ops:
  0.6 1.5 %copy_pieces.1 = bf16[4,32,16,128]{3,2,1,0:T(8,128)(2,1)} custom-call(bf16[4,1024]{1,0:T(4,128)(2,1)} %k_ref.3, bf16[4,1024]{1,0:T(4,128)(2,1)} %v_ref.3), custom_call_target="tpu_custom_call" | custom-call | tf_op jit(solution)/shard_map/copy_pieces/pallas_call | solution.py:429
  2.2 11.5 %all-to-all-start = ((bf16[128,16,128]{2,1,0:T(8,128)(2,1)}), bf16[128,16,128]{2,1,0:T(8,128)(2,1)S(1)}, u32[]{:S(2)}, u32[]{:S(2)}) async-start(bf16[128,16,128]{2,1,0:T(8,128)(2,1)} %bitcast), calls=%async_computation | async-start | bytes 1048576 | tf_op jit(solution)/shard_map/all_to_all | solution.py:436
  13.7 0.0 copy-start
  13.7 7.8 %own_forward.1 = (f32[16,128,512]{2,1,0:T(8,128)}, f32[16,8,512]{2,1,0:T(8,128)}, f32[16,512]{1,0:T(8,128)}) custom-call(bf16[512,2048]{1,0:T(8,128)(2,1)} %q_ref.5, bf16[512,256]{1,0:T(8,128)(2,1)} %k_ref.5, bf16[512,256]{1,0:T(8,128)(2,1)} %v_ref.5), custom_call_target="tpu_custom_call" | custom-call | flops 2147483648 | bytes 8388608 | tf_op jit(solution)/shard_map/own_forward/pallas_call | solution.py:334
  21.5 5.8 %all-to-all-done.near_ref = bf16[128,16,128]{2,1,0:T(8,128)(2,1)S(1)} async-done(((bf16[128,16,128]{2,1,0:T(8,128)(2,1)}), bf16[128,16,128]{2,1,0:T(8,128)(2,1)S(1)}, u32[]{:S(2)}, u32[]{:S(2)}) %all-to-all-start) | async-done | bytes 524320 | tf_op jit(solution)/shard_map/all_to_all | solution.py:436
  27.3 0.0 copy-done
  27.3 22.4 %shared_pass.1 = (bf16[512,2048]{1,0:T(8,128)(2,1)}, f32[16,128,512]{2,1,0:T(8,128)}, f32[16,8,512]{2,1,0:T(8,128)}, bf16[128,16,128]{2,1,0:T(8,128)(2,1)}) custom-call(s32[32]{0:T(128)S(1)} %copy-done, bf16[512,2048]{1,0:T(8,128)(2,1)} %q_ref.5, bf16[512,2048]{1,0:T(8,128)(2,1)} %g_ref.3, bf16[128,16,128]{2,1,0:T(8,128)(2,1)S(1)} %all-to-all-done.near_ref, ...), custom_call_target="tpu_custom_call" | custom-call | flops 6442450944 | bytes 16777216 | tf_op jit(solution)/shard_map/shared_pass/pallas_call | solution.py:361
  49.6 4.6 %all-to-all-start.1 = ((bf16[128,16,128]{2,1,0:T(8,128)(2,1)}), bf16[128,16,128]{2,1,0:T(8,128)(2,1)S(1)}, u32[]{:S(2)}, u32[]{:S(2)}) async-start(bf16[128,16,128]{2,1,0:T(8,128)(2,1)} %get-tuple-element.27), calls=%async_computation.1 | async-start | bytes 1048576 | tf_op jit(solution)/shard_map/all_to_all | solution.py:444
  54.2 11.5 %own_backward.1 = (bf16[512,2048]{1,0:T(8,128)(2,1)}, bf16[512,256]{1,0:T(8,128)(2,1)}, bf16[512,256]{1,0:T(8,128)(2,1)}) custom-call(s32[32]{0:T(128)S(1)} %copy-done, bf16[512,2048]{1,0:T(8,128)(2,1)} %q_ref.5, bf16[512,2048]{1,0:T(8,128)(2,1)} %g_ref.3, bf16[512,256]{1,0:T(8,128)(2,1)} %k_ref.5, bf16[512,256]{1,0:T(8,128)(2,1)} %v_ref.5, ...), custom_call_target="tpu_custom_call" | custom-call | flops 5368709120 | bytes 12582912 | tf_op jit(solution)/shard_map/own_backward/pallas_call | solution.py:398
  65.8 2.2 %all-to-all-done.1 = bf16[128,16,128]{2,1,0:T(8,128)(2,1)S(1)} async-done(((bf16[128,16,128]{2,1,0:T(8,128)(2,1)}), bf16[128,16,128]{2,1,0:T(8,128)(2,1)S(1)}, u32[]{:S(2)}, u32[]{:S(2)}) %all-to-all-start.1) | async-done | bytes 524320 | tf_op jit(solution)/shard_map/all_to_all | solution.py:444
  68.0 0.7 %add_terms.1 = (bf16[4,1024]{1,0:T(4,128)(2,1)}, bf16[4,1024]{1,0:T(4,128)(2,1)}) custom-call(bf16[4,32,16,128]{3,2,1,0:T(8,128)(2,1)S(1)} %bitcast.2), custom_call_target="tpu_custom_call" | custom-call | tf_op jit(solution)/shard_map/add_terms/pallas_call | solution.py:448
Async XLA Ops:
  2.2 25.1 %all-to-all-start = ((bf16[128,16,128]{2,1,0:T(8,128)(2,1)}), bf16[128,16,128]{2,1,0:T(8,128)(2,1)S(1)}, u32[]{:S(2)}, u32[]{:S(2)}) async-start(bf16[128,16,128]{2,1,0:T(8,128)(2,1)} %bitcast), calls=%async_computation | async-start | bytes 1048576 | tf_op jit(solution)/shard_map/all_to_all | solution.py:436
  13.7 13.6 %copy-start = (s32[32]{0:T(128)S(1)}, s32[32]{0:T(128)}, u32[]{:S(2)}) copy-start(s32[32]{0:T(128)} %lengths_ref.3) | copy-start | bytes 388
  49.6 18.3 %all-to-all-start.1 = ((bf16[128,16,128]{2,1,0:T(8,128)(2,1)}), bf16[128,16,128]{2,1,0:T(8,128)(2,1)S(1)}, u32[]{:S(2)}, u32[]{:S(2)}) async-start(bf16[128,16,128]{2,1,0:T(8,128)(2,1)} %get-tuple-element.27), calls=%async_computation.1 | async-start | bytes 1048576 | tf_op jit(solution)/shard_map/all_to_all | solution.py:444

commit v5 on v4

--- a/solution.py
+++ b/solution.py
@@ -271,7 +271,7 @@
                 at = (share * groups + one) * HD
                 parts.append(ref[:, at : at + HD].astype(F32))
         piece = jnp.concatenate(parts, axis=0).astype(BF16)
-        out_ref[share] = jnp.broadcast_to(piece[None], (copies,) + piece.shape)
+        out_ref[shares - 1 - share] = jnp.broadcast_to(piece[None], (copies,) + piece.shape)
 
 
 def add_terms(terms_ref, k_ref, v_ref):
@@ -279,7 +279,7 @@
     shares = terms_ref.shape[0]
     groups = width // shares // HD
     for share in range(shares):
-        total = jnp.sum(terms_ref[share].astype(F32), axis=0)
+        total = jnp.sum(terms_ref[shares - 1 - share].astype(F32), axis=0)
         for which, ref in enumerate((k_ref, v_ref)):
             for one in range(groups):
                 row = (which * groups + one) * tokens
@@ -433,7 +433,10 @@
         name="copy_pieces",
     )(prompt_keys, prompt_values)
     pieces = pieces.reshape(shares * copies, chunk, HD)
-    arrived = lax.all_to_all(pieces, axes, split_axis=0, concat_axis=0, tiled=True)
+    backward = [list(reversed(range(shares * copies)))]
+    arrived = lax.all_to_all(pieces, axes, split_axis=0, concat_axis=0, tiled=True,
+        axis_index_groups=backward,
+    )
 
     q, resp_k, resp_v, grad_out = in_hbm(q, resp_k, resp_v, grad_out)
     mixed, stats, limit = in_hbm(*run_own_forward(q, resp_k, resp_v))
@@ -441,7 +444,9 @@
         lengths, q, grad_out, arrived, mixed, stats, limit
     )
     part, back = in_hbm(part, back)
-    terms = lax.all_to_all(terms, axes, split_axis=0, concat_axis=0, tiled=True)
+    terms = lax.all_to_all(terms, axes, split_axis=0, concat_axis=0, tiled=True,
+        axis_index_groups=backward,
+    )
     query_grads, key_grads, value_grads = run_own_backward(
         lengths, q, grad_out, resp_k, resp_v, part, back
     )

time: 69 us -> 68.9 us (level)
  starting transfers between devices: 16.1 us -> 15.3 us
    all_to_all x2, starting transfers between devices: 16.1 us -> 15.3 us  [the longest x1 11.5 us: on_device(): lax.all_to_all(pieces, axes, split_axis=0, concat_axis=0, tiled=True, axi...]
where the time goes in v5:
time: 68.9 us; the launch traced here: 68.5 us
  Pallas kernels  43.9 us (64%)
  starting transfers between devices  15.3 us (22%)
  waiting for transfers between devices  8.69 us (13%)
    pallas_call x1, Pallas kernels, run_shared(): pl.pallas_call(functools.partial(shared_pass, per_group=heads // groups),...  22.4 us
    pallas_call x1, Pallas kernels, run_own_backward(): pl.pallas_call(functools.partial(own_backward, per_group=heads // groups)...  11.5 us
    all_to_all x1, starting transfers between devices, on_device(): lax.all_to_all(pieces, axes, split_axis=0, concat_axis=0, tiled=True, axi...  11.5 us
    pallas_call x1, Pallas kernels, run_own_forward(): pl.pallas_call(functools.partial(own_forward, per_group=heads // groups),...  7.76 us
    all_to_all x1, waiting for transfers between devices, on_device(): lax.all_to_all(pieces, axes, split_axis=0, concat_axis=0, tiled=True, axi...  6.18 us
    all_to_all x1, starting transfers between devices, on_device(): lax.all_to_all(terms, axes, split_axis=0, concat_axis=0, tiled=True, axis...  3.78 us
    all_to_all x1, waiting for transfers between devices, on_device(): lax.all_to_all(terms, axes, split_axis=0, concat_axis=0, tiled=True, axis...  2.51 us
    pallas_call x1, Pallas kernels, on_device(): pl.pallas_call(copy_pieces, out_shape=shape((shares, copies, chunk, HD),...  1.55 us
  transfers between devices with their start and end apart: 2, of which 2 were waited for; matrix products, arithmetic and copies ran while one was open for 0% of the time, Pallas kernels for 28%

profile of v5, /device:TPU:1, one launch (start us, length us, event | category | flops | bytes accessed | tf_op | source)
XLA Modules:
  0.0 68.5 jit_solution(4961424616101239475)
XLA Ops:
  0.6 1.5 %copy_pieces.1 = bf16[4,32,16,128]{3,2,1,0:T(8,128)(2,1)} custom-call(bf16[4,1024]{1,0:T(4,128)(2,1)} %k_ref.3, bf16[4,1024]{1,0:T(4,128)(2,1)} %v_ref.3), custom_call_target="tpu_custom_call" | custom-call | tf_op jit(solution)/shard_map/copy_pieces/pallas_call | solution.py:429
  2.2 11.5 %all-to-all-start = ((bf16[128,16,128]{2,1,0:T(8,128)(2,1)}), bf16[128,16,128]{2,1,0:T(8,128)(2,1)S(1)}, u32[]{:S(2)}, u32[]{:S(2)}) async-start(bf16[128,16,128]{2,1,0:T(8,128)(2,1)} %bitcast), calls=%async_computation | async-start | bytes 1048576 | tf_op jit(solution)/shard_map/all_to_all | solution.py:437
  13.7 0.0 copy-start
  13.7 7.8 %own_forward.1 = (f32[16,128,512]{2,1,0:T(8,128)}, f32[16,8,512]{2,1,0:T(8,128)}, f32[16,512]{1,0:T(8,128)}) custom-call(bf16[512,2048]{1,0:T(8,128)(2,1)} %q_ref.5, bf16[512,256]{1,0:T(8,128)(2,1)} %k_ref.5, bf16[512,256]{1,0:T(8,128)(2,1)} %v_ref.5), custom_call_target="tpu_custom_call" | custom-call | flops 2147483648 | bytes 8388608 | tf_op jit(solution)/shard_map/own_forward/pallas_call | solution.py:334
  21.5 6.2 %all-to-all-done.near_ref = bf16[128,16,128]{2,1,0:T(8,128)(2,1)S(1)} async-done(((bf16[128,16,128]{2,1,0:T(8,128)(2,1)}), bf16[128,16,128]{2,1,0:T(8,128)(2,1)S(1)}, u32[]{:S(2)}, u32[]{:S(2)}) %all-to-all-start) | async-done | bytes 524320 | tf_op jit(solution)/shard_map/all_to_all | solution.py:437
  27.6 0.0 copy-done
  27.6 22.4 %shared_pass.1 = (bf16[512,2048]{1,0:T(8,128)(2,1)}, f32[16,128,512]{2,1,0:T(8,128)}, f32[16,8,512]{2,1,0:T(8,128)}, bf16[128,16,128]{2,1,0:T(8,128)(2,1)}) custom-call(s32[32]{0:T(128)S(1)} %copy-done, bf16[512,2048]{1,0:T(8,128)(2,1)} %q_ref.5, bf16[512,2048]{1,0:T(8,128)(2,1)} %g_ref.3, bf16[128,16,128]{2,1,0:T(8,128)(2,1)S(1)} %all-to-all-done.near_ref, ...), custom_call_target="tpu_custom_call" | custom-call | flops 6442450944 | bytes 16777216 | tf_op jit(solution)/shard_map/shared_pass/pallas_call | solution.py:361
  50.0 3.8 %all-to-all-start.1 = ((bf16[128,16,128]{2,1,0:T(8,128)(2,1)}), bf16[128,16,128]{2,1,0:T(8,128)(2,1)S(1)}, u32[]{:S(2)}, u32[]{:S(2)}) async-start(bf16[128,16,128]{2,1,0:T(8,128)(2,1)} %get-tuple-element.27), calls=%async_computation.1 | async-start | bytes 1048576 | tf_op jit(solution)/shard_map/all_to_all | solution.py:447
  53.8 11.5 %own_backward.1 = (bf16[512,2048]{1,0:T(8,128)(2,1)}, bf16[512,256]{1,0:T(8,128)(2,1)}, bf16[512,256]{1,0:T(8,128)(2,1)}) custom-call(s32[32]{0:T(128)S(1)} %copy-done, bf16[512,2048]{1,0:T(8,128)(2,1)} %q_ref.5, bf16[512,2048]{1,0:T(8,128)(2,1)} %g_ref.3, bf16[512,256]{1,0:T(8,128)(2,1)} %k_ref.5, bf16[512,256]{1,0:T(8,128)(2,1)} %v_ref.5, ...), custom_call_target="tpu_custom_call" | custom-call | flops 5368709120 | bytes 12582912 | tf_op jit(solution)/shard_map/own_backward/pallas_call | solution.py:398
  65.3 2.5 %all-to-all-done.1 = bf16[128,16,128]{2,1,0:T(8,128)(2,1)S(1)} async-done(((bf16[128,16,128]{2,1,0:T(8,128)(2,1)}), bf16[128,16,128]{2,1,0:T(8,128)(2,1)S(1)}, u32[]{:S(2)}, u32[]{:S(2)}) %all-to-all-start.1) | async-done | bytes 524320 | tf_op jit(solution)/shard_map/all_to_all | solution.py:447
  67.8 0.7 %add_terms.1 = (bf16[4,1024]{1,0:T(4,128)(2,1)}, bf16[4,1024]{1,0:T(4,128)(2,1)}) custom-call(bf16[4,32,16,128]{3,2,1,0:T(8,128)(2,1)S(1)} %bitcast.2), custom_call_target="tpu_custom_call" | custom-call | tf_op jit(solution)/shard_map/add_terms/pallas_call | solution.py:453
Async XLA Ops:
  2.2 25.5 %all-to-all-start = ((bf16[128,16,128]{2,1,0:T(8,128)(2,1)}), bf16[128,16,128]{2,1,0:T(8,128)(2,1)S(1)}, u32[]{:S(2)}, u32[]{:S(2)}) async-start(bf16[128,16,128]{2,1,0:T(8,128)(2,1)} %bitcast), calls=%async_computation | async-start | bytes 1048576 | tf_op jit(solution)/shard_map/all_to_all | solution.py:437
  13.7 14.0 %copy-start = (s32[32]{0:T(128)S(1)}, s32[32]{0:T(128)}, u32[]{:S(2)}) copy-start(s32[32]{0:T(128)} %lengths_ref.3) | copy-start | bytes 388
  50.0 17.8 %all-to-all-start.1 = ((bf16[128,16,128]{2,1,0:T(8,128)(2,1)}), bf16[128,16,128]{2,1,0:T(8,128)(2,1)S(1)}, u32[]{:S(2)}, u32[]{:S(2)}) async-start(bf16[128,16,128]{2,1,0:T(8,128)(2,1)} %get-tuple-element.27), calls=%async_computation.1 | async-start | bytes 1048576 | tf_op jit(solution)/shard_map/all_to_all | solution.py:447

commit v6 on v5

--- a/solution.py
+++ b/solution.py
@@ -262,7 +262,7 @@
 
 def copy_pieces(k_ref, v_ref, out_ref):
     tokens, width = k_ref.shape
-    shares, copies = out_ref.shape[:2]
+    copies, shares = out_ref.shape[:2]
     groups = width // shares // HD
     for share in range(shares):
         parts = []
@@ -271,15 +271,15 @@
                 at = (share * groups + one) * HD
                 parts.append(ref[:, at : at + HD].astype(F32))
         piece = jnp.concatenate(parts, axis=0).astype(BF16)
-        out_ref[shares - 1 - share] = jnp.broadcast_to(piece[None], (copies,) + piece.shape)
+        out_ref[:, shares - 1 - share] = jnp.broadcast_to(piece[None], (copies,) + piece.shape)
 
 
 def add_terms(terms_ref, k_ref, v_ref):
     tokens, width = k_ref.shape
-    shares = terms_ref.shape[0]
+    shares = terms_ref.shape[1]
     groups = width // shares // HD
     for share in range(shares):
-        total = jnp.sum(terms_ref[shares - 1 - share].astype(F32), axis=0)
+        total = jnp.sum(terms_ref[:, shares - 1 - share].astype(F32), axis=0)
         for which, ref in enumerate((k_ref, v_ref)):
             for one in range(groups):
                 row = (which * groups + one) * tokens
@@ -428,12 +428,14 @@
     prompt_keys, prompt_values = in_hbm(prompt_keys, prompt_values)
     pieces = pl.pallas_call(
         copy_pieces,
-        out_shape=shape((shares, copies, chunk, HD), BF16),
+        out_shape=shape((copies, shares, chunk, HD), BF16),
         compiler_params=pltpu.CompilerParams(vmem_limit_bytes=VMEM_LIMIT),
         name="copy_pieces",
     )(prompt_keys, prompt_values)
     pieces = pieces.reshape(shares * copies, chunk, HD)
-    backward = [list(reversed(range(shares * copies)))]
+    backward = [
+        [p * copies + r for r in reversed(range(copies)) for p in reversed(range(shares))]
+    ]
     arrived = lax.all_to_all(pieces, axes, split_axis=0, concat_axis=0, tiled=True,
         axis_index_groups=backward,
     )
@@ -455,7 +457,7 @@
         out_shape=[shape((tokens, width), BF16)] * 2,
         compiler_params=pltpu.CompilerParams(vmem_limit_bytes=VMEM_LIMIT),
         name="add_terms",
-    )(terms.reshape(shares, copies, chunk, HD))
+    )(terms.reshape(copies, shares, chunk, HD))
     return attended, query_grads, key_grads, value_grads, prompt_kg, prompt_vg
 
 

time: 68.9 us -> 68.4 us (level)
  waiting for transfers between devices: 8.69 us -> 7.65 us
where the time goes in v6:
time: 68.4 us; the launch traced here: 68.1 us
  Pallas kernels  43.9 us (64%)
  starting transfers between devices  15.9 us (23%)
  waiting for transfers between devices  7.65 us (11%)
    pallas_call x1, Pallas kernels, run_shared(): pl.pallas_call(functools.partial(shared_pass, per_group=heads // groups),...  22.4 us
    pallas_call x1, Pallas kernels, run_own_backward(): pl.pallas_call(functools.partial(own_backward, per_group=heads // groups)...  11.5 us
    all_to_all x1, starting transfers between devices, on_device(): lax.all_to_all(pieces, axes, split_axis=0, concat_axis=0, tiled=True, axi...  11.5 us
    pallas_call x1, Pallas kernels, run_own_forward(): pl.pallas_call(functools.partial(own_forward, per_group=heads // groups),...  7.76 us
    all_to_all x1, waiting for transfers between devices, on_device(): lax.all_to_all(pieces, axes, split_axis=0, concat_axis=0, tiled=True, axi...  5.69 us
    all_to_all x1, starting transfers between devices, on_device(): lax.all_to_all(terms, axes, split_axis=0, concat_axis=0, tiled=True, axis...  4.38 us
    all_to_all x1, waiting for transfers between devices, on_device(): lax.all_to_all(terms, axes, split_axis=0, concat_axis=0, tiled=True, axis...  1.96 us
    pallas_call x1, Pallas kernels, on_device(): pl.pallas_call(copy_pieces, out_shape=shape((copies, shares, chunk, HD),...  1.57 us
  transfers between devices with their start and end apart: 2, of which 2 were waited for; matrix products, arithmetic and copies ran while one was open for 0% of the time, Pallas kernels for 28%

profile of v6, /device:TPU:1, one launch (start us, length us, event | category | flops | bytes accessed | tf_op | source)
XLA Modules:
  0.0 68.1 jit_solution(9645910269074491393)
XLA Ops:
  0.6 1.6 %copy_pieces.1 = bf16[32,4,16,128]{3,2,1,0:T(8,128)(2,1)} custom-call(bf16[4,1024]{1,0:T(4,128)(2,1)} %k_ref.3, bf16[4,1024]{1,0:T(4,128)(2,1)} %v_ref.3), custom_call_target="tpu_custom_call" | custom-call | tf_op jit(solution)/shard_map/copy_pieces/pallas_call | solution.py:429
  2.2 11.5 %all-to-all-start = ((bf16[128,16,128]{2,1,0:T(8,128)(2,1)}), bf16[128,16,128]{2,1,0:T(8,128)(2,1)S(1)}, u32[]{:S(2)}, u32[]{:S(2)}) async-start(bf16[128,16,128]{2,1,0:T(8,128)(2,1)} %bitcast), calls=%async_computation | async-start | bytes 1048576 | tf_op jit(solution)/shard_map/all_to_all | solution.py:439
  13.7 0.0 copy-start
  13.7 7.8 %own_forward.1 = (f32[16,128,512]{2,1,0:T(8,128)}, f32[16,8,512]{2,1,0:T(8,128)}, f32[16,512]{1,0:T(8,128)}) custom-call(bf16[512,2048]{1,0:T(8,128)(2,1)} %q_ref.5, bf16[512,256]{1,0:T(8,128)(2,1)} %k_ref.5, bf16[512,256]{1,0:T(8,128)(2,1)} %v_ref.5), custom_call_target="tpu_custom_call" | custom-call | flops 2147483648 | bytes 8388608 | tf_op jit(solution)/shard_map/own_forward/pallas_call | solution.py:334
  21.5 5.7 %all-to-all-done.near_ref = bf16[128,16,128]{2,1,0:T(8,128)(2,1)S(1)} async-done(((bf16[128,16,128]{2,1,0:T(8,128)(2,1)}), bf16[128,16,128]{2,1,0:T(8,128)(2,1)S(1)}, u32[]{:S(2)}, u32[]{:S(2)}) %all-to-all-start) | async-done | bytes 524320 | tf_op jit(solution)/shard_map/all_to_all | solution.py:439
  27.2 0.0 copy-done
  27.2 22.4 %shared_pass.1 = (bf16[512,2048]{1,0:T(8,128)(2,1)}, f32[16,128,512]{2,1,0:T(8,128)}, f32[16,8,512]{2,1,0:T(8,128)}, bf16[128,16,128]{2,1,0:T(8,128)(2,1)}) custom-call(s32[32]{0:T(128)S(1)} %copy-done, bf16[512,2048]{1,0:T(8,128)(2,1)} %q_ref.5, bf16[512,2048]{1,0:T(8,128)(2,1)} %g_ref.3, bf16[128,16,128]{2,1,0:T(8,128)(2,1)S(1)} %all-to-all-done.near_ref, ...), custom_call_target="tpu_custom_call" | custom-call | flops 6442450944 | bytes 16777216 | tf_op jit(solution)/shard_map/shared_pass/pallas_call | solution.py:361
  49.5 4.4 %all-to-all-start.1 = ((bf16[128,16,128]{2,1,0:T(8,128)(2,1)}), bf16[128,16,128]{2,1,0:T(8,128)(2,1)S(1)}, u32[]{:S(2)}, u32[]{:S(2)}) async-start(bf16[128,16,128]{2,1,0:T(8,128)(2,1)} %get-tuple-element.27), calls=%async_computation.1 | async-start | bytes 1048576 | tf_op jit(solution)/shard_map/all_to_all | solution.py:449
  53.9 11.5 %own_backward.1 = (bf16[512,2048]{1,0:T(8,128)(2,1)}, bf16[512,256]{1,0:T(8,128)(2,1)}, bf16[512,256]{1,0:T(8,128)(2,1)}) custom-call(s32[32]{0:T(128)S(1)} %copy-done, bf16[512,2048]{1,0:T(8,128)(2,1)} %q_ref.5, bf16[512,2048]{1,0:T(8,128)(2,1)} %g_ref.3, bf16[512,256]{1,0:T(8,128)(2,1)} %k_ref.5, bf16[512,256]{1,0:T(8,128)(2,1)} %v_ref.5, ...), custom_call_target="tpu_custom_call" | custom-call | flops 5368709120 | bytes 12582912 | tf_op jit(solution)/shard_map/own_backward/pallas_call | solution.py:398
  65.4 2.0 %all-to-all-done.1 = bf16[128,16,128]{2,1,0:T(8,128)(2,1)S(1)} async-done(((bf16[128,16,128]{2,1,0:T(8,128)(2,1)}), bf16[128,16,128]{2,1,0:T(8,128)(2,1)S(1)}, u32[]{:S(2)}, u32[]{:S(2)}) %all-to-all-start.1) | async-done | bytes 524320 | tf_op jit(solution)/shard_map/all_to_all | solution.py:449
  67.4 0.7 %add_terms.1 = (bf16[4,1024]{1,0:T(4,128)(2,1)}, bf16[4,1024]{1,0:T(4,128)(2,1)}) custom-call(bf16[32,4,16,128]{3,2,1,0:T(8,128)(2,1)S(1)} %bitcast.2), custom_call_target="tpu_custom_call" | custom-call | tf_op jit(solution)/shard_map/add_terms/pallas_call | solution.py:455
Async XLA Ops:
  2.2 25.0 %all-to-all-start = ((bf16[128,16,128]{2,1,0:T(8,128)(2,1)}), bf16[128,16,128]{2,1,0:T(8,128)(2,1)S(1)}, u32[]{:S(2)}, u32[]{:S(2)}) async-start(bf16[128,16,128]{2,1,0:T(8,128)(2,1)} %bitcast), calls=%async_computation | async-start | bytes 1048576 | tf_op jit(solution)/shard_map/all_to_all | solution.py:439
  13.7 13.5 %copy-start = (s32[32]{0:T(128)S(1)}, s32[32]{0:T(128)}, u32[]{:S(2)}) copy-start(s32[32]{0:T(128)} %lengths_ref.3) | copy-start | bytes 388
  49.5 17.9 %all-to-all-start.1 = ((bf16[128,16,128]{2,1,0:T(8,128)(2,1)}), bf16[128,16,128]{2,1,0:T(8,128)(2,1)S(1)}, u32[]{:S(2)}, u32[]{:S(2)}) async-start(bf16[128,16,128]{2,1,0:T(8,128)(2,1)} %get-tuple-element.27), calls=%async_computation.1 | async-start | bytes 1048576 | tf_op jit(solution)/shard_map/all_to_all | solution.py:449
